TPU v7x, 32 devices: a whole 2x2x4 slice. The times are simulated.
32 devices in a mesh: clip: 8 (over z, core), row: 4 (over y, x).
Axes of the slice: x: 2, y: 2, z: 4, core: 2. Of those that a mesh axis runs over, the one named last changes fastest.
Arguments:
- latents: float32 [8, 9, 8, 16, 128], P('clip', None, 'row'), may hold values from -6 to 6
- noise: float32 [8, 9, 8, 16, 128], P('clip', None, 'row'), may hold values from -6 to 6
- levels: int32 [8, 9], P('clip'), may hold values from 0 to 999
- w_patch: float32 [128, 1024], P('clip'), may hold values from -0.5 to 0.5
- w_level: float32 [256, 1024], P('clip', 'row'), may hold values from -0.375 to 0.375
- w_adapt: float32 [1024, 8192], P('row', 'clip'), may hold values from -0.1875 to 0.1875
- w_project: float32 [1024, 3, 1024], P('clip', None, 'row'), may hold values from -0.1875 to 0.1875
- w_output: float32 [1024, 1024], P('row', 'clip'), may hold values from -1.5 to 1.5
- w_gateup: float32 [1024, 2, 4096], P('clip', None, 'row'), may hold values from -0.1875 to 0.1875
- w_down: float32 [4096, 1024], P('row', 'clip'), may hold values from -0.09375 to 0.09375
- w_head: float32 [1024, 128], P('clip'), may hold values from -0.1875 to 0.1875
- first_patch: float32 [128, 1024], P('clip'), may hold values from -2.3841858e-07 to 2.3841858e-07
- first_level: float32 [256, 1024], P('clip', 'row'), may hold values from -2.3841858e-07 to 2.3841858e-07
- first_adapt: float32 [1024, 8192], P('row', 'clip'), may hold values from -2.3841858e-07 to 2.3841858e-07
- first_project: float32 [1024, 3, 1024], P('clip', None, 'row'), may hold values from -2.3841858e-07 to 2.3841858e-07
- first_output: float32 [1024, 1024], P('row', 'clip'), may hold values from -2.3841858e-07 to 2.3841858e-07
- first_gateup: float32 [1024, 2, 4096], P('clip', None, 'row'), may hold values from -2.3841858e-07 to 2.3841858e-07
- first_down: float32 [4096, 1024], P('row', 'clip'), may hold values from -2.3841858e-07 to 2.3841858e-07
- first_head: float32 [1024, 128], P('clip'), may hold values from -2.3841858e-07 to 2.3841858e-07
- second_patch: float32 [128, 1024], P('clip'), may hold values from 8.189922e-15 to 3.2759687e-14
- second_level: float32 [256, 1024], P('clip', 'row'), may hold values from 8.189922e-15 to 3.2759687e-14
- second_adapt: float32 [1024, 8192], P('row', 'clip'), may hold values from 8.189922e-15 to 3.2759687e-14
- second_project: float32 [1024, 3, 1024], P('clip', None, 'row'), may hold values from 8.189922e-15 to 3.2759687e-14
- second_output: float32 [1024, 1024], P('row', 'clip'), may hold values from 8.189922e-15 to 3.2759687e-14
- second_gateup: float32 [1024, 2, 4096], P('clip', None, 'row'), may hold values from 1.0276328e-15 to 4.094961e-15
- second_down: float32 [4096, 1024], P('row', 'clip'), may hold values from 8.189922e-15 to 3.2759687e-14
- second_head: float32 [1024, 128], P('clip'), may hold values from 8.189922e-15 to 3.2759687e-14
Outputs:
- loss_sum: float32 [], replicated
- weight_sum: float32 [], replicated
- grad_norm: float32 [], replicated
- new_patch: float32 [128, 1024], P('clip')
- new_level: float32 [256, 1024], P('clip', 'row')
- new_adapt: float32 [1024, 8192], P('row', 'clip')
- new_project: float32 [1024, 3, 1024], P('clip', None, 'row')
- new_output: float32 [1024, 1024], P('row', 'clip')
- new_gateup: float32 [1024, 2, 4096], P('clip', None, 'row')
- new_down: float32 [4096, 1024], P('row', 'clip')
- new_head: float32 [1024, 128], P('clip')
- mean_patch: float32 [128, 1024], P('clip')
- mean_level: float32 [256, 1024], P('clip', 'row')
- mean_adapt: float32 [1024, 8192], P('row', 'clip')
- mean_project: float32 [1024, 3, 1024], P('clip', None, 'row')
- mean_output: float32 [1024, 1024], P('row', 'clip')
- mean_gateup: float32 [1024, 2, 4096], P('clip', None, 'row')
- mean_down: float32 [4096, 1024], P('row', 'clip')
- mean_head: float32 [1024, 128], P('clip')
- square_patch: float32 [128, 1024], P('clip')
- square_level: float32 [256, 1024], P('clip', 'row')
- square_adapt: float32 [1024, 8192], P('row', 'clip')
- square_project: float32 [1024, 3, 1024], P('clip', None, 'row')
- square_output: float32 [1024, 1024], P('row', 'clip')
- square_gateup: float32 [1024, 2, 4096], P('clip', None, 'row')
- square_down: float32 [4096, 1024], P('row', 'clip')
- square_head: float32 [1024, 128], P('clip')
All inputs are finite; a program needn't handle non-finite values.
Results may differ from a plain program's by a relative error of at most 0.0094.
Values may be sent and summed in bfloat16 or wider, within the bound.
A program may use at most 192 MiB of HBM per device.

v0:
```python
import math

import jax
import jax.numpy as jnp
from jax import lax
from jax.sharding import PartitionSpec as P

D = 1024
HEADS = 16
HSIZE = 64
TF = 256
LEVELS = 1000
STEP = 3


norm_eps = 1e-06
clip_level = 0.002
learn_rate = 0.03
beta_one = 0.9
beta_two = 0.95
decay_rate = 0.1
adam_eps = 1e-08


def forward_dot(left, right):
    return jnp.dot(left, right, preferred_element_type=jnp.float32)


def outer_product(left, right):
    return lax.dot_general(
        left, right, (((0,), (0,)), ((), ())), preferred_element_type=jnp.float32
    )


def times_transposed(left, right):
    return lax.dot_general(
        left, right, (((1,), (1,)), ((), ())), preferred_element_type=jnp.float32
    )


def frequencies(number):
    return jnp.exp(-math.log(10000.0) * jnp.arange(number, dtype=jnp.float32) / number)


def rotary_tables(frames, row_count, col_count, row_offset, half):
    frame_part = half // 4
    row_part = 3 * half // 8
    col_part = half - frame_part - row_part
    frame_pos = jnp.arange(frames, dtype=jnp.float32)
    row_pos = jnp.arange(row_count, dtype=jnp.float32) + row_offset
    col_pos = jnp.arange(col_count, dtype=jnp.float32)
    shape = (frames, row_count, col_count)
    angle = jnp.concatenate(
        [
            jnp.broadcast_to(
                frame_pos[:, None, None, None] * frequencies(frame_part), shape + (frame_part,)
            ),
            jnp.broadcast_to(
                row_pos[None, :, None, None] * frequencies(row_part), shape + (row_part,)
            ),
            jnp.broadcast_to(
                col_pos[None, None, :, None] * frequencies(col_part), shape + (col_part,)
            ),
        ],
        -1,
    )
    angle = angle.reshape(frames, row_count * col_count, 1, half)
    return (jnp.cos(angle), jnp.sin(angle))


def rotate(values, cosine, sine):
    half = values.shape[-1] // 2
    first_half = values[..., :half]
    second_half = values[..., half:]
    return jnp.concatenate(
        [first_half * cosine - second_half * sine, first_half * sine + second_half * cosine], -1
    )


def rotate_back(grads, cosine, sine):
    half = grads.shape[-1] // 2
    first_half = grads[..., :half]
    second_half = grads[..., half:]
    return jnp.concatenate(
        [first_half * cosine + second_half * sine, second_half * cosine - first_half * sine], -1
    )


def modulate(stream, shift, scale):
    centre = stream - jnp.mean(stream, -1, keepdims=True)
    spread = jnp.mean(centre * centre, -1, keepdims=True)
    return centre * lax.rsqrt(spread + norm_eps) * (1.0 + scale) + shift


def norm_back(stream, shift, scale, grad_out):
    unused, pull = jax.vjp(modulate, stream, shift, scale)
    return pull(grad_out)


def noise_plan(levels):
    ratio = levels.astype(jnp.float32) / LEVELS
    alpha_bar = jnp.cos((ratio + 0.008) / 1.008 * (math.pi / 2)) ** 2
    weight = jnp.minimum(1.0, 5.0 * (1.0 - alpha_bar) / alpha_bar)
    return (alpha_bar, weight)


def level_embedding(levels, half):
    angle = levels.astype(jnp.float32)[..., None] * frequencies(half)
    return jnp.concatenate([jnp.cos(angle), jnp.sin(angle)], -1)


def block_pieces(query, key, value, index, block_rows, frame_rows):
    seq = query.shape[1]
    blocks = seq // block_rows
    clip_at = index // blocks
    start = index % blocks * block_rows
    query_whole = lax.dynamic_index_in_dim(query, clip_at, 0, keepdims=False)
    query_block = lax.dynamic_slice_in_dim(query_whole, start, block_rows, 0)
    key_whole = lax.dynamic_index_in_dim(key, clip_at, 0, keepdims=False)
    value_whole = lax.dynamic_index_in_dim(value, clip_at, 0, keepdims=False)
    key_frame = jnp.arange(seq, dtype=jnp.int32) // frame_rows
    query_frame = (start + jnp.arange(block_rows, dtype=jnp.int32)) // frame_rows
    allowed = key_frame[None, None, :] <= query_frame[None, :, None]
    scores = jnp.einsum("qhe,khe->hqk", query_block, key_whole, preferred_element_type=jnp.float32)
    scores = jnp.where(allowed, scores, -1e30)
    return (clip_at, start, query_block, key_whole, value_whole, allowed, scores)


def local_attend(query, key, value, frame_rows):
    clip_count, seq, head_count, head_size = query.shape
    block_rows = 3 * frame_rows

    def attend_block(index):
        unused_clip, unused_start, unused_query, unused_key, value_whole, allowed, scores = (
            block_pieces(query, key, value, index, block_rows, frame_rows)
        )
        row_max = jnp.max(scores, -1)
        exponent = jnp.where(allowed, jnp.exp(scores - row_max[..., None]), 0.0)
        row_total = jnp.sum(exponent, -1)
        mixed = jnp.einsum(
            "hqk,khe->qhe",
            exponent.astype(jnp.bfloat16),
            value_whole,
            preferred_element_type=jnp.float32,
        )
        return (mixed / jnp.transpose(row_total)[:, :, None], row_max + jnp.log(row_total))

    count = clip_count * (seq // block_rows)
    mixed, log_total = lax.map(attend_block, jnp.arange(count, dtype=jnp.int32))
    return (mixed.reshape(clip_count, seq, head_count, head_size), log_total)


def local_attend_back(query, key, value, log_total, delta, grad_out, frame_rows):
    clip_count, seq, head_count, head_size = query.shape
    block_rows = 3 * frame_rows
    count = clip_count * (seq // block_rows)
    delta_blocks = jnp.transpose(delta.reshape(count, block_rows, head_count), (0, 2, 1))

    def back_block(index, running):
        grad_query, grad_key, grad_value = running
        clip_at, start, query_block, key_whole, value_whole, allowed, scores = block_pieces(
            query, key, value, index, block_rows, frame_rows
        )
        grad_whole = lax.dynamic_index_in_dim(grad_out, clip_at, 0, keepdims=False)
        grad_block = lax.dynamic_slice_in_dim(grad_whole, start, block_rows, 0)
        total_block = lax.dynamic_index_in_dim(log_total, index, 0, keepdims=False)
        delta_block = lax.dynamic_index_in_dim(delta_blocks, index, 0, keepdims=False)
        probs = jnp.where(allowed, jnp.exp(scores - total_block[..., None]), 0.0)
        value_grad = jnp.einsum(
            "hqk,qhe->khe",
            probs.astype(jnp.bfloat16),
            grad_block,
            preferred_element_type=jnp.float32,
        )
        grad_probs = jnp.einsum(
            "qhe,khe->hqk", grad_block, value_whole, preferred_element_type=jnp.float32
        )
        grad_scores = (probs * (grad_probs - delta_block[..., None])).astype(jnp.bfloat16)
        query_grad = jnp.einsum(
            "hqk,khe->qhe", grad_scores, key_whole, preferred_element_type=jnp.float32
        )
        key_grad = jnp.einsum(
            "hqk,qhe->khe", grad_scores, query_block, preferred_element_type=jnp.float32
        )
        grad_query = lax.dynamic_update_slice(grad_query, query_grad[None], (clip_at, start, 0, 0))
        grad_key = grad_key.at[clip_at].add(key_grad)
        grad_value = grad_value.at[clip_at].add(value_grad)
        return (grad_query, grad_key, grad_value)

    zeros = jnp.zeros((clip_count, seq, head_count, head_size), jnp.float32)
    return lax.fori_loop(0, count, back_block, (zeros, zeros, zeros))


def adam_update(master, first, second, grad):
    first_new = beta_one * first + (1.0 - beta_one) * grad
    second_new = beta_two * second + (1.0 - beta_two) * grad * grad
    first_hat = first_new / (1.0 - beta_one**STEP)
    second_hat = second_new / (1.0 - beta_two**STEP)
    master_new = master - learn_rate * (
        first_hat / (jnp.sqrt(second_hat) + adam_eps) + decay_rate * master
    )
    return (master_new, first_new, second_new)


def on_device(
    latents,
    noise,
    levels,
    w_patch,
    w_level,
    w_adapt,
    w_project,
    w_output,
    w_gateup,
    w_down,
    w_head,
    first_patch,
    first_level,
    first_adapt,
    first_project,
    first_output,
    first_gateup,
    first_down,
    first_head,
    second_patch,
    second_level,
    second_adapt,
    second_project,
    second_output,
    second_gateup,
    second_down,
    second_head,
):
    parts = lax.axis_size("row")
    gathered = (
        lax.all_gather(w_level.astype(jnp.bfloat16), "clip", axis=0, tiled=True),
        lax.all_gather(w_adapt.astype(jnp.bfloat16), "clip", axis=1, tiled=True),
        lax.all_gather(w_project.astype(jnp.bfloat16), "clip", axis=0, tiled=True),
        lax.all_gather(w_output.astype(jnp.bfloat16), "clip", axis=1, tiled=True),
        lax.all_gather(w_gateup.astype(jnp.bfloat16), "clip", axis=0, tiled=True),
        lax.all_gather(w_down.astype(jnp.bfloat16), "clip", axis=1, tiled=True),
        lax.all_gather(w_patch.astype(jnp.bfloat16), "clip", axis=0, tiled=True),
        lax.all_gather(w_head.astype(jnp.bfloat16), "clip", axis=0, tiled=True),
    )
    level_cut, adapt_cut, project_cut, output_cut, gateup_cut, down_cut, patch_full, head_full = (
        gathered
    )
    clip_count, frames, row_count, col_count, features = latents.shape
    local_frame = row_count * col_count
    whole_frame = local_frame * parts
    seq = frames * whole_frame
    token_count = clip_count * frames * local_frame
    head_count = HEADS // parts
    head_width = head_count * HSIZE
    hidden_cut = gateup_cut.shape[2]
    project_flat = project_cut.reshape(D, 3 * head_width)
    gateup_flat = gateup_cut.reshape(D, 2 * hidden_cut)
    score_scale = HSIZE ** (-0.5)
    alpha_bar, frame_weight = noise_plan(levels)
    latent_flat = latents.reshape(clip_count, frames, local_frame, features)
    noise_flat = noise.reshape(clip_count, frames, local_frame, features)
    noisy = (
        jnp.sqrt(alpha_bar)[:, :, None, None] * latent_flat
        + jnp.sqrt(1.0 - alpha_bar)[:, :, None, None] * noise_flat
    )
    inputs = noisy.astype(jnp.bfloat16).reshape(token_count, features)
    embedded = (
        level_embedding(levels, TF // 2).astype(jnp.bfloat16).reshape(clip_count * frames, TF)
    )
    level_pre = forward_dot(embedded, level_cut)
    condition = jax.nn.silu(level_pre).astype(jnp.bfloat16)
    adapt = lax.psum(forward_dot(condition, adapt_cut), "row")
    adapt = adapt.reshape(clip_count, frames, 8, 1, D)
    stream = forward_dot(inputs, patch_full).reshape(clip_count, frames, local_frame, D)
    normed_one = modulate(stream, adapt[:, :, 0], adapt[:, :, 1]).astype(jnp.bfloat16)
    one_full = lax.all_gather(normed_one, "row", axis=2, tiled=True).reshape(clip_count * seq, D)
    projected = forward_dot(one_full, project_flat).reshape(
        clip_count, frames, whole_frame, 3, head_count, HSIZE
    )
    cosine, sine = rotary_tables(frames, row_count * parts, col_count, 0.0, HSIZE // 2)
    shape_four = (clip_count, seq, head_count, HSIZE)
    query = (
        (rotate(projected[:, :, :, 0], cosine, sine) * score_scale)
        .astype(jnp.bfloat16)
        .reshape(shape_four)
    )
    key = rotate(projected[:, :, :, 1], cosine, sine).astype(jnp.bfloat16).reshape(shape_four)
    value = projected[:, :, :, 2].astype(jnp.bfloat16).reshape(shape_four)
    attended, log_total = local_attend(query, key, value, whole_frame)
    attended_low = attended.astype(jnp.bfloat16).reshape(clip_count * seq, head_width)
    branch_part = forward_dot(attended_low, output_cut).reshape(clip_count, frames, whole_frame, D)
    branch = lax.psum_scatter(branch_part, "row", scatter_dimension=2, tiled=True)
    stream_mid = stream + adapt[:, :, 2] * branch
    normed_two = modulate(stream_mid, adapt[:, :, 3], adapt[:, :, 4]).astype(jnp.bfloat16)
    two_full = lax.all_gather(normed_two, "row", axis=2, tiled=True).reshape(clip_count * seq, D)
    gate_up = forward_dot(two_full, gateup_flat)
    gate_part = gate_up[:, :hidden_cut]
    up_part = gate_up[:, hidden_cut:]
    active = (jax.nn.gelu(gate_part) * up_part).astype(jnp.bfloat16)
    feed_part = forward_dot(active, down_cut).reshape(clip_count, frames, whole_frame, D)
    feed = lax.psum_scatter(feed_part, "row", scatter_dimension=2, tiled=True)
    stream_top = stream_mid + adapt[:, :, 5] * feed
    normed_end = (
        modulate(stream_top, adapt[:, :, 6], adapt[:, :, 7])
        .astype(jnp.bfloat16)
        .reshape(token_count, D)
    )
    predicted = forward_dot(normed_end, head_full).reshape(
        clip_count, frames, local_frame, features
    )
    missed = predicted - noise_flat
    loss_local = jnp.sum(frame_weight[:, :, None] * jnp.mean(missed * missed, -1))
    weight_local = jnp.sum(frame_weight) * local_frame
    grad_pred = (2.0 / features * frame_weight[:, :, None, None] * missed).astype(jnp.bfloat16)
    grad_pred = grad_pred.reshape(token_count, features)
    grad_head = outer_product(normed_end, grad_pred)
    grad_end = times_transposed(grad_pred, head_full).reshape(clip_count, frames, local_frame, D)
    grad_top, grad_shift_c, grad_scale_c = norm_back(
        stream_top, adapt[:, :, 6], adapt[:, :, 7], grad_end
    )
    grad_gate_b = jnp.sum(grad_top * feed, 2, keepdims=True)
    grad_feed = (grad_top * adapt[:, :, 5]).astype(jnp.bfloat16)
    feed_full = lax.all_gather(grad_feed, "row", axis=2, tiled=True).reshape(clip_count * seq, D)
    grad_down = outer_product(active, feed_full)
    grad_active = times_transposed(feed_full, down_cut)
    unused, pull = jax.vjp(lambda gate_in, up_in: jax.nn.gelu(gate_in) * up_in, gate_part, up_part)
    grad_gate, grad_upper = pull(grad_active)
    gateup_rows = jnp.concatenate([grad_gate, grad_upper], 1).astype(jnp.bfloat16)
    grad_gateup = outer_product(two_full, gateup_rows).reshape(D, 2, hidden_cut)
    two_part = times_transposed(gateup_rows, gateup_flat).reshape(
        clip_count, frames, whole_frame, D
    )
    grad_two = lax.psum_scatter(two_part, "row", scatter_dimension=2, tiled=True)
    grad_mid_norm, grad_shift_b, grad_scale_b = norm_back(
        stream_mid, adapt[:, :, 3], adapt[:, :, 4], grad_two
    )
    grad_mid = grad_top + grad_mid_norm
    grad_gate_a = jnp.sum(grad_mid * branch, 2, keepdims=True)
    grad_branch = (grad_mid * adapt[:, :, 2]).astype(jnp.bfloat16)
    branch_full = lax.all_gather(grad_branch, "row", axis=2, tiled=True).reshape(
        clip_count * seq, D
    )
    grad_output = outer_product(attended_low, branch_full)
    grad_attended = (
        times_transposed(branch_full, output_cut).astype(jnp.bfloat16).reshape(shape_four)
    )
    delta = jnp.sum(grad_attended.astype(jnp.float32) * attended, -1)
    grad_query, grad_key, grad_value = local_attend_back(
        query, key, value, log_total, delta, grad_attended, whole_frame
    )
    shape_six = (clip_count, frames, whole_frame, head_count, HSIZE)
    query_back = rotate_back(grad_query.reshape(shape_six) * score_scale, cosine, sine)
    key_back = rotate_back(grad_key.reshape(shape_six), cosine, sine)
    grad_projected = jnp.stack([query_back, key_back, grad_value.reshape(shape_six)], axis=3)
    grad_projected = grad_projected.astype(jnp.bfloat16).reshape(clip_count * seq, 3 * head_width)
    grad_project = outer_product(one_full, grad_projected).reshape(D, 3, head_width)
    one_part = times_transposed(grad_projected, project_flat).reshape(
        clip_count, frames, whole_frame, D
    )
    grad_one = lax.psum_scatter(one_part, "row", scatter_dimension=2, tiled=True)
    grad_low_norm, grad_shift_a, grad_scale_a = norm_back(
        stream, adapt[:, :, 0], adapt[:, :, 1], grad_one
    )
    grad_stream = (grad_mid + grad_low_norm).astype(jnp.bfloat16).reshape(token_count, D)
    grad_patch = outer_product(inputs, grad_stream)
    adapt_rows = jnp.concatenate(
        [
            grad_shift_a,
            grad_scale_a,
            grad_gate_a,
            grad_shift_b,
            grad_scale_b,
            grad_gate_b,
            grad_shift_c,
            grad_scale_c,
        ],
        axis=2,
    )
    adapt_rows = adapt_rows.reshape(clip_count * frames, 8 * D)
    adapt_total, patch_total, head_total = lax.psum((adapt_rows, grad_patch, grad_head), "row")
    adapt_low = adapt_total.astype(jnp.bfloat16)
    grad_adapt = outer_product(condition, adapt_low)
    grad_condition = times_transposed(adapt_low, adapt_cut)
    unused, pull = jax.vjp(jax.nn.silu, level_pre)
    grad_level_pre = pull(grad_condition)[0].astype(jnp.bfloat16)
    grad_level = outer_product(embedded, grad_level_pre)
    shards = (
        lax.psum_scatter(grad_level, "clip", scatter_dimension=0, tiled=True),
        lax.psum_scatter(grad_adapt, "clip", scatter_dimension=1, tiled=True),
        lax.psum_scatter(grad_project, "clip", scatter_dimension=0, tiled=True),
        lax.psum_scatter(grad_output, "clip", scatter_dimension=1, tiled=True),
        lax.psum_scatter(grad_gateup, "clip", scatter_dimension=0, tiled=True),
        lax.psum_scatter(grad_down, "clip", scatter_dimension=1, tiled=True),
        lax.psum_scatter(patch_total, "clip", scatter_dimension=0, tiled=True),
        lax.psum_scatter(head_total, "clip", scatter_dimension=0, tiled=True),
    )
    owner = (lax.axis_index("row") == 0).astype(jnp.float32)
    squares_local = sum((jnp.sum(shard * shard) for shard in shards[:6]))
    squares_local = squares_local + owner * (
        jnp.sum(shards[6] * shards[6]) + jnp.sum(shards[7] * shards[7])
    )
    loss_sum, weight_sum, squares_total = lax.psum(
        (loss_local, weight_local, squares_local), ("clip", "row")
    )
    grad_norm = jnp.sqrt(squares_total) / weight_sum
    factor = jnp.minimum(1.0, clip_level / (grad_norm + 1e-06)) / weight_sum
    ordered = (
        shards[6],
        shards[0],
        shards[1],
        shards[2],
        shards[3],
        shards[4],
        shards[5],
        shards[7],
    )
    masters = (w_patch, w_level, w_adapt, w_project, w_output, w_gateup, w_down, w_head)
    firsts = (
        first_patch,
        first_level,
        first_adapt,
        first_project,
        first_output,
        first_gateup,
        first_down,
        first_head,
    )
    seconds = (
        second_patch,
        second_level,
        second_adapt,
        second_project,
        second_output,
        second_gateup,
        second_down,
        second_head,
    )
    results = [
        adam_update(master, first, second, shard * factor)
        for master, first, second, shard in zip(masters, firsts, seconds, ordered)
    ]
    news = [item[0] for item in results]
    means = [item[1] for item in results]
    squares = [item[2] for item in results]
    return (
        loss_sum,
        weight_sum,
        grad_norm,
        news[0],
        news[1],
        news[2],
        news[3],
        news[4],
        news[5],
        news[6],
        news[7],
        means[0],
        means[1],
        means[2],
        means[3],
        means[4],
        means[5],
        means[6],
        means[7],
        squares[0],
        squares[1],
        squares[2],
        squares[3],
        squares[4],
        squares[5],
        squares[6],
        squares[7],
    )


def solution(mesh):
    return jax.shard_map(
        on_device,
        mesh=mesh,
        in_specs=(
            P("clip", None, "row", None, None),
            P("clip", None, "row", None, None),
            P("clip", None),
            P("clip", None),
            P("clip", "row"),
            P("row", "clip"),
            P("clip", None, "row"),
            P("row", "clip"),
            P("clip", None, "row"),
            P("row", "clip"),
            P("clip", None),
            P("clip", None),
            P("clip", "row"),
            P("row", "clip"),
            P("clip", None, "row"),
            P("row", "clip"),
            P("clip", None, "row"),
            P("row", "clip"),
            P("clip", None),
            P("clip", None),
            P("clip", "row"),
            P("row", "clip"),
            P("clip", None, "row"),
            P("row", "clip"),
            P("clip", None, "row"),
            P("row", "clip"),
            P("clip", None),
        ),
        out_specs=(
            P(),
            P(),
            P(),
            P("clip", None),
            P("clip", "row"),
            P("row", "clip"),
            P("clip", None, "row"),
            P("row", "clip"),
            P("clip", None, "row"),
            P("row", "clip"),
            P("clip", None),
            P("clip", None),
            P("clip", "row"),
            P("row", "clip"),
            P("clip", None, "row"),
            P("row", "clip"),
            P("clip", None, "row"),
            P("row", "clip"),
            P("clip", None),
            P("clip", None),
            P("clip", "row"),
            P("row", "clip"),
            P("clip", None, "row"),
            P("row", "clip"),
            P("clip", None, "row"),
            P("row", "clip"),
            P("clip", None),
        ),
        check_vma=False,
    )
```

profile of v0, /device:TPU:0, one launch (start us, length us, event | category | flops | bytes accessed | tf_op | source)
XLA Modules:
  0.0 1297.6 jit_solution(5154636472147013677)
XLA Ops:
  9.5 15.7 %all_gather.37 = bf16[256,256]{1,0:T(8,128)(2,1)S(1)} all-gather(bf16[32,256]{1,0:T(8,128)(2,1)S(1)} %convert_element_type.214), channel_id=1, replica_groups=mesh['clip'=8,'row'=4] {'clip'}, dimensions={0}, use_global_device_ids=true | all-gather | bytes 147456 | tf_op jit(solution)/shard_map/all_gather | solution.py:236
  26.1 34.1 %all-gather.9.cloned.1.call-done = bf16[256,8192]{1,0:T(8,128)(2,1)} async-done(((bf16[256,1024]{1,0:T(8,128)(2,1)}), bf16[256,8192]{1,0:T(8,128)(2,1)}) %all-gather.9.cloned.1.call-update) | async-done | bytes 4194320 | tf_op jit(solution)/shard_map/all_gather | solution.py:237
  66.5 14.2 %all_gather.36 = bf16[128,1024]{1,0:T(8,128)(2,1)S(1)} all-gather(bf16[16,1024]{1,0:T(8,128)(2,1)S(1)} %convert_element_type.213), channel_id=1, replica_groups=mesh['clip'=8,'row'=4] {'clip'}, dimensions={0}, use_global_device_ids=true | all-gather | bytes 294912 | tf_op jit(solution)/shard_map/all_gather | solution.py:242
  82.3 24.1 %all-reduce.6.cloned.1.call-done = f32[1,9,8,1,1024]{4,2,1,3,0:T(8,128)} async-done(((f32[1,9,8,1,1024]{4,2,1,3,0:T(8,128)}), f32[1,9,8,1,1024]{4,2,1,3,0:T(8,128)}) %all-reduce.6.cloned.1.call-update) | async-done | bytes 294928 | tf_op jit(solution)/shard_map/psum | solution.py:272
  114.8 18.5 %all_gather.41 = bf16[256,1024]{1,0:T(8,128)(2,1)} all-gather(bf16[256,128]{1,0:T(8,128)(2,1)S(1)} %convert_element_type.223), channel_id=1, replica_groups=mesh['clip'=8,'row'=4] {'clip'}, dimensions={1}, use_global_device_ids=true | all-gather | bytes 589824 | tf_op jit(solution)/shard_map/all_gather | solution.py:239
  133.3 6.0 all-gather.13.cloned.1.call-done
  139.2 39.6 %all-gather.11.cloned.1.call-done = bf16[1,9,128,1024]{3,2,1,0:T(8,128)(2,1)} async-done(((bf16[1,9,32,1024]{3,2,1,0:T(8,128)(2,1)}), bf16[1,9,128,1024]{3,2,1,0:T(8,128)(2,1)}) %all-gather.11.cloned.1.call-update) | async-done | bytes 2359312 | tf_op jit(solution)/shard_map/all_gather | solution.py:276
  178.8 4.4 fusion.82
  189.5 26.7 %while.38 = (s32[]{:T(128)}, f32[3,384,4,64]{1,3,2,0:T(8,128)}, f32[3,4,384]{2,1,0:T(4,128)}, s32[3]{0:T(128)S(1)}, bf16[1,1152,4,64]{1,3,2,0:T(8,128)(2,1)S(1)}...) while((s32[]{:T(128)}, f32[3,384,4,64]{1,3,2,0:T(8,128)}, ...), condition=%wide.region_6.7_spmd, body=%wide.region_3.6_spmd.sunk | while | flops 471234048 | bytes 24835320 | solution.py:149
  222.7 4.1 convolution_bitcast_fusion.3
  230.6 53.5 %reduce-scatter.13.cloned.1.call-done = f32[1,9,32,1024]{3,2,1,0:T(8,128)} async-done(((f32[1,9,128,1024]{3,2,1,0:T(8,128)}), f32[1,9,32,1024]{3,2,1,0:T(8,128)}) %reduce-scatter.13.cloned.1.call-update) | async-done | bytes 1179664 | tf_op jit(solution)/shard_map/reduce_scatter | solution.py:292
  288.2 45.1 %all-gather.17.cloned.1.call-done = bf16[1024,2,1024]{2,1,0:T(2,128)(2,1)} async-done(((bf16[128,2,1024]{2,1,0:T(2,128)(2,1)}), bf16[1024,2,1024]{2,1,0:T(2,128)(2,1)}) %all-gather.17.cloned.1.call-update) | async-done | bytes 4194320 | tf_op jit(solution)/shard_map/all_gather | solution.py:240
  333.4 5.5 copy.191
  338.9 33.3 %all-gather.15.cloned.1.call-done = bf16[1,9,128,1024]{3,2,1,0:T(8,128)(2,1)} async-done(((bf16[1,9,32,1024]{3,2,1,0:T(8,128)(2,1)}), bf16[1,9,128,1024]{3,2,1,0:T(8,128)(2,1)}) %all-gather.15.cloned.1.call-update) | async-done | bytes 2359312 | tf_op jit(solution)/shard_map/all_gather | solution.py:295
  372.2 7.6 fusion.153
  386.1 19.2 %all-gather.19.cloned.1.call-done = bf16[1024,1024]{1,0:T(8,128)(2,1)} async-done(((bf16[1024,128]{1,0:T(8,128)(2,1)}), bf16[1024,1024]{1,0:T(8,128)(2,1)}) %all-gather.19.cloned.1.call-update) | async-done | bytes 2097168 | tf_op jit(solution)/shard_map/all_gather | solution.py:241
  405.3 7.0 fusion.154
  413.2 15.4 %all_gather.45 = bf16[1024,128]{1,0:T(8,128)(2,1)} all-gather(bf16[128,128]{1,0:T(8,128)(2,1)S(1)} %convert_element_type.229), channel_id=1, replica_groups=mesh['clip'=8,'row'=4] {'clip'}, dimensions={0}, use_global_device_ids=true | all-gather | bytes 294912 | tf_op jit(solution)/shard_map/all_gather | solution.py:243
  429.9 38.8 %reduce-scatter.15.cloned.1.call-done = f32[1,9,32,1024]{3,2,1,0:T(8,128)} async-done(((f32[1,9,128,1024]{3,2,1,0:T(8,128)}), f32[1,9,32,1024]{3,2,1,0:T(8,128)}) %reduce-scatter.15.cloned.1.call-update) | async-done | bytes 1179664 | tf_op jit(solution)/shard_map/reduce_scatter | solution.py:301
  477.2 7.9 reshape.1263
  485.1 29.2 %all-gather.21.cloned.1.call-done = bf16[1,9,128,1024]{3,2,1,0:T(8,128)(2,1)} async-done(((bf16[1,9,32,1024]{3,2,1,0:T(8,128)(2,1)}), bf16[1,9,128,1024]{3,2,1,0:T(8,128)(2,1)}) %all-gather.21.cloned.1.call-update) | async-done | bytes 2359312 | tf_op jit(solution)/shard_map/all_gather | solution.py:323
  514.3 10.2 fusion.72
  526.7 6.8 fusion.79
  533.6 57.2 %reduce-scatter.17.cloned.1.call-done = f32[1,9,32,1024]{3,2,1,0:T(8,128)} async-done(((f32[1,9,128,1024]{3,2,1,0:T(8,128)}), f32[1,9,32,1024]{3,2,1,0:T(8,128)}) %reduce-scatter.17.cloned.1.call-update) | async-done | bytes 1179664 | tf_op jit(solution)/shard_map/reduce_scatter | solution.py:333
  599.0 37.6 %all-gather.23.cloned.1.call-done = bf16[1,9,128,1024]{3,2,1,0:T(8,128)(2,1)} async-done(((bf16[1,9,32,1024]{3,2,1,0:T(8,128)(2,1)}), bf16[1,9,128,1024]{3,2,1,0:T(8,128)(2,1)}) %all-gather.23.cloned.1.call-update) | async-done | bytes 2359312 | tf_op jit(solution)/shard_map/all_gather | solution.py:340
  643.3 60.5 %while.39 = (s32[]{:T(128)}, f32[1,1152,4,64]{1,3,2,0:T(8,128)}, f32[1,1152,4,64]{1,3,2,0:T(8,128)}, f32[1,1152,4,64]{1,3,2,0:T(8,128)}, bf16[1,1152,4,64]{1,3,2...) while((s32[]{:T(128)}, f32[1,1152,4,64]{1,3,2,0:T(8,128)}, ...), condition=%wide.region_26.27_spmd.clone, body=%wide.region_24.26_spmd.clone.sunk | while | flops 1147075584 | bytes 113751752 | solution.py:191
  672.1 4.1 fusion.226
  679.3 4.0 fusion.227
  692.6 4.1 fusion.226
  699.8 4.0 fusion.227
  716.1 4.2 convolution_bitcast_fusion.2
  723.5 54.1 %reduce-scatter.19.cloned.1.call-done = f32[1,9,32,1024]{3,2,1,0:T(8,128)} async-done(((f32[1,9,128,1024]{3,2,1,0:T(8,128)}), f32[1,9,32,1024]{3,2,1,0:T(8,128)}) %reduce-scatter.19.cloned.1.call-update) | async-done | bytes 1179664 | tf_op jit(solution)/shard_map/reduce_scatter | solution.py:360
  782.4 6.1 fusion.159
  792.3 5.2 maximum_bitcast_fusion
  797.4 6.9 copy.171
  804.3 10.2 fusion.158
  819.3 4.0 fusion.156
  825.4 27.0 %all-reduce.9 = bf16[9,8192]{1,0:T(8,128)(2,1)S(1)} all-reduce(f32[9,8192]{1,0:T(8,128)S(1)} %bitcast.360), channel_id=1, replica_groups=mesh['clip'=8,'row'=4] {'row'}, use_global_device_ids=true, to_apply=%region_36.37 | all-reduce | flops 73728 | bytes 442368 | tf_op jit(solution)/shard_map/psum | solution.py:380
  852.4 4.3 fusion.120
  857.6 4.5 fusion.105
  864.7 29.0 %reduce-scatter.31.cloned.1.call-done = f32[1024,128]{1,0:T(8,128)} async-done(((f32[1024,1024]{1,0:T(8,128)}), f32[1024,128]{1,0:T(8,128)}) %reduce-scatter.31.cloned.1.call-update) | async-done | bytes 524304 | tf_op jit(solution)/shard_map/reduce_scatter | solution.py:393
  895.5 31.6 %reduce-scatter.27.cloned.1.call-done = f32[256,128]{1,0:T(8,128)} async-done(((f32[256,1024]{1,0:T(8,128)}), f32[256,128]{1,0:T(8,128)}) %reduce-scatter.27.cloned.1.call-update) | async-done | bytes 131088 | tf_op jit(solution)/shard_map/reduce_scatter | solution.py:391
  928.6 88.5 %reduce-scatter.29.cloned.1.call-done = f32[128,2,1024]{2,0,1:T(8,128)} async-done(((f32[1024,2,1024]{2,0,1:T(8,128)}), f32[128,2,1024]{2,0,1:T(8,128)}) %reduce-scatter.29.cloned.1.call-update) | async-done | bytes 1048592 | tf_op jit(solution)/shard_map/reduce_scatter | solution.py:392
  1019.3 38.9 %reduce-scatter.25.cloned.1.call-done = f32[128,3,256]{2,0,1:T(8,128)} async-done(((f32[1024,3,256]{2,0,1:T(8,128)}), f32[128,3,256]{2,0,1:T(8,128)}) %reduce-scatter.25.cloned.1.call-update) | async-done | bytes 393232 | tf_op jit(solution)/shard_map/reduce_scatter | solution.py:390
  1059.9 30.6 %reduce-scatter.21.cloned.1.call-done = f32[32,256]{1,0:T(8,128)} async-done(((f32[256,256]{1,0:T(8,128)}), f32[32,256]{1,0:T(8,128)}) %reduce-scatter.21.cloned.1.call-update) | async-done | bytes 32784 | tf_op jit(solution)/shard_map/reduce_scatter | solution.py:388
  1091.8 41.7 %all-reduce.8.cloned.1.call-done = (f32[16,1024]{1,0:T(8,128)}, f32[128,128]{1,0:T(8,128)}) async-done(((f32[16,1024]{1,0:T(8,128)}, f32[128,128]{1,0:T(8,128)}), (f32[16,1024]{1,0:T(8,128)}, f32[128,128]{1,0:T(8,128)})) %all-reduce.8.cloned.1.call-update) | async-done | bytes 131088 | tf_op jit(solution)/shard_map/psum | solution.py:380
  1137.8 87.8 %reduce-scatter.23.cloned.1.call-done = f32[256,1024]{1,0:T(8,128)} async-done(((f32[256,8192]{1,0:T(8,128)}), f32[256,1024]{1,0:T(8,128)}) %reduce-scatter.23.cloned.1.call-update) | async-done | bytes 1048592 | tf_op jit(solution)/shard_map/reduce_scatter | solution.py:389
  1231.6 38.4 %all-reduce = (f32[]{:T(128)}, f32[]{:T(128)}, f32[]{:T(128)}) all-reduce(f32[]{:T(128)} %multiply_reduce_fusion.20, f32[]{:T(128)S(6)} %mul.1102, f32[]{:T(128)S(6)} %add.622), channel_id=1, replica_groups=mesh['clip'=8,'row'=4] {'clip','row'}, use_global_device_ids=true, to_apply=%region_15.16 | all-reduce | flops 3 | bytes 24 | tf_op jit(solution)/shard_map/psum | solution.py:402
  (588 shorter events, 205.3 us)
Async XLA Ops:
  7.2 18.0 %copy-start.141 = (s32[1,9]{1,0:T(1,128)S(1)}, s32[1,9]{1,0:T(1,128)}, u32[]{:S(2)}) copy-start(s32[1,9]{1,0:T(1,128)} %param.37) | copy-start | bytes 112
  7.2 52.9 %all-gather.9.cloned.1.call-start = ((), (), s32[]{:S(2)}) async-start(), calls=%async_computation.12 | async-start | bytes 4718592 | tf_op jit(solution)/shard_map/all_gather | solution.py:237
  9.4 97.0 %all-reduce.6.cloned.1.call-start = ((), (), s32[]{:S(2)}) async-start(), calls=%async_computation.13 | async-start | bytes 589824 | tf_op jit(solution)/shard_map/psum | solution.py:272
  26.1 34.1 %copy-start.79 = (f32[9,256]{1,0:T(8,128)}, f32[9,256]{1,0:T(8,128)S(1)}, u32[]{:S(2)}) copy-start(f32[9,256]{1,0:T(8,128)S(1)} %fusion.127) | copy-start | bytes 27652
  63.0 17.7 %copy-start.66 = (f32[1,9,2,16,128]{4,3,2,1,0:T(8,128)S(1)}, f32[1,9,2,16,128]{4,3,2,1,0:T(8,128)}, u32[]{:S(2)}) copy-start(f32[1,9,2,16,128]{4,3,2,1,0:T(8,128)} %param.36) | copy-start | bytes 442372
  63.0 17.7 %copy-start.69 = (f32[1,9,2,16,128]{4,3,2,1,0:T(8,128)S(1)}, f32[1,9,2,16,128]{4,3,2,1,0:T(8,128)}, u32[]{:S(2)}) copy-start(f32[1,9,2,16,128]{4,3,2,1,0:T(8,128)} %param.35) | copy-start | bytes 442372
  64.1 75.2 %all-gather.13.cloned.1.call-start = ((), (), s32[]{:S(2)}) async-start(), calls=%async_computation.15 | async-start | bytes 1769472 | tf_op jit(solution)/shard_map/all_gather | solution.py:238
  65.0 113.8 %all-gather.11.cloned.1.call-start = ((), (), s32[]{:S(2)}) async-start(), calls=%async_computation.14 | async-start | bytes 2949120 | tf_op jit(solution)/shard_map/all_gather | solution.py:276
  81.2 202.9 %copy-start.4 = (f32[288,1024]{1,0:T(8,128)}, f32[288,1024]{1,0:T(8,128)S(1)}, u32[]{:S(2)}) copy-start(f32[288,1024]{1,0:T(8,128)S(1)} %get-tuple-element.765) | copy-start | bytes 3538948
  81.3 30.1 %copy-start.96 = (f32[9,32]{1,0:T(8,128)}, f32[9,32]{1,0:T(8,128)S(1)}, u32[]{:S(2)}) copy-start(f32[9,32]{1,0:T(8,128)S(1)} %div.303) | copy-start | bytes 3460
  82.3 29.2 %copy-start.104 = (f32[9,32]{1,0:T(8,128)}, f32[9,32]{1,0:T(8,128)S(1)}, u32[]{:S(2)}) copy-start(f32[9,32]{1,0:T(8,128)S(1)} %rsqrt.36) | copy-start | bytes 3460
  111.5 172.6 %reduce-scatter.13.cloned.1.call-start = ((), (), s32[]{:S(2)}) async-start(), calls=%async_computation.16 | async-start | bytes 5898240 | tf_op jit(solution)/shard_map/reduce_scatter | solution.py:292
  114.6 69.0 %copy-start.54 = (f32[9,128,32]{1,2,0:T(8,128)}, f32[9,128,32]{1,2,0:T(8,128)S(1)}, u32[]{:S(2)}) copy-start(f32[9,128,32]{1,2,0:T(8,128)S(1)} %copy.133) | copy-start | bytes 442372
  114.8 68.8 %copy-start.56 = (f32[9,128,32]{1,2,0:T(8,128)}, f32[9,128,32]{1,2,0:T(8,128)S(1)}, u32[]{:S(2)}) copy-start(f32[9,128,32]{1,2,0:T(8,128)S(1)} %copy.134) | copy-start | bytes 442372
  226.9 106.5 %all-gather.17.cloned.1.call-start = ((), (), s32[]{:S(2)}) async-start(), calls=%async_computation.18 | async-start | bytes 4718592 | tf_op jit(solution)/shard_map/all_gather | solution.py:240
  229.3 142.9 %all-gather.15.cloned.1.call-start = ((), (), s32[]{:S(2)}) async-start(), calls=%async_computation.17 | async-start | bytes 2949120 | tf_op jit(solution)/shard_map/all_gather | solution.py:295
  287.1 118.2 %all-gather.19.cloned.1.call-start = ((), (), s32[]{:S(2)}) async-start(), calls=%async_computation.19 | async-start | bytes 2359296 | tf_op jit(solution)/shard_map/all_gather | solution.py:241
  287.9 180.8 %reduce-scatter.15.cloned.1.call-start = ((), (), s32[]{:S(2)}) async-start(), calls=%async_computation.20 | async-start | bytes 5898240 | tf_op jit(solution)/shard_map/reduce_scatter | solution.py:301
  412.4 16.2 %copy-start.100 = (f32[1,9,1,1,1024]{4,2,1,3,0:T(1,128)S(1)}, f32[1,9,1,1,1024]{4,2,1,3,0:T(1,128)}, u32[]{:S(2)}) copy-start(f32[1,9,1,1,1024]{4,2,1,3,0:T(1,128)} %get-tuple-element.750) | copy-start | bytes 110596
  412.4 16.9 %copy-start.98 = (f32[1,9,1,1,1024]{4,2,1,3,0:T(1,128)S(1)}, f32[1,9,1,1,1024]{4,2,1,3,0:T(1,128)}, u32[]{:S(2)}) copy-start(f32[1,9,1,1,1024]{4,2,1,3,0:T(1,128)} %get-tuple-element.746) | copy-start | bytes 110596
  412.4 16.9 %copy-start.99 = (f32[1,9,1,1,1024]{4,2,1,3,0:T(1,128)S(1)}, f32[1,9,1,1,1024]{4,2,1,3,0:T(1,128)}, u32[]{:S(2)}) copy-start(f32[1,9,1,1,1024]{4,2,1,3,0:T(1,128)} %get-tuple-element.747) | copy-start | bytes 110596
  412.4 101.9 %all-gather.21.cloned.1.call-start = ((), (), s32[]{:S(2)}) async-start(), calls=%async_computation.21 | async-start | bytes 2949120 | tf_op jit(solution)/shard_map/all_gather | solution.py:323
  476.7 114.1 %reduce-scatter.17.cloned.1.call-start = ((), (), s32[]{:S(2)}) async-start(), calls=%async_computation.22 | async-start | bytes 5898240 | tf_op jit(solution)/shard_map/reduce_scatter | solution.py:333
  514.3 12.4 copy-start.28
  533.5 57.2 %copy-start.49 = (f32[9,1024]{1,0:T(8,128)S(1)}, f32[9,1024]{1,0:T(8,128)}, u32[]{:S(2)}) copy-start(f32[9,1024]{1,0:T(8,128)} %get-tuple-element.769) | copy-start | bytes 110596
  533.5 103.0 %all-gather.23.cloned.1.call-start = ((), (), s32[]{:S(2)}) async-start(), calls=%async_computation.23 | async-start | bytes 2949120 | tf_op jit(solution)/shard_map/all_gather | solution.py:340
  596.9 39.6 %copy-start.41 = (bf16[256,1024]{1,0:T(8,128)(2,1)S(1)}, bf16[256,1024]{1,0:T(8,128)(2,1)}, u32[]{:S(2)}) copy-start(bf16[256,1024]{1,0:T(8,128)(2,1)} %all_gather.41) | copy-start | bytes 1572868
  598.9 178.7 %reduce-scatter.19.cloned.1.call-start = ((), (), s32[]{:S(2)}) async-start(), calls=%async_computation.24 | async-start | bytes 5898240 | tf_op jit(solution)/shard_map/reduce_scatter | solution.py:360
  720.4 136.5 %reduce-scatter.35.cloned.1.call-start = ((), (), s32[]{:S(2)}) async-start(), calls=%async_computation.32 | async-start | bytes 589824 | tf_op jit(solution)/shard_map/reduce_scatter | solution.py:395
  722.0 55.6 %copy-start.5 = (f32[288,1024]{1,0:T(8,128)S(1)}, f32[288,1024]{1,0:T(8,128)}, u32[]{:S(2)}) copy-start(f32[288,1024]{1,0:T(8,128)} %copy-done.4) | copy-start | bytes 3538948
  722.0 55.6 %copy-start.46 = (f32[9,1024]{1,0:T(8,128)S(1)}, f32[9,1024]{1,0:T(8,128)}, u32[]{:S(2)}) copy-start(f32[9,1024]{1,0:T(8,128)} %copy-done.45) | copy-start | bytes 110596
  722.0 55.5 %copy-start.97 = (f32[9,32]{1,0:T(8,128)S(1)}, f32[9,32]{1,0:T(8,128)}, u32[]{:S(2)}) copy-start(f32[9,32]{1,0:T(8,128)} %copy-done.96) | copy-start | bytes 3460
  723.4 55.8 %copy-start.123 = (f32[9,32]{1,0:T(8,128)S(1)}, f32[9,32]{1,0:T(8,128)}, u32[]{:S(2)}) copy-start(f32[9,32]{1,0:T(8,128)} %copy-done.122) | copy-start | bytes 3460
  723.4 55.9 %copy-start.105 = (f32[9,32]{1,0:T(8,128)S(1)}, f32[9,32]{1,0:T(8,128)}, u32[]{:S(2)}) copy-start(f32[9,32]{1,0:T(8,128)} %copy-done.104) | copy-start | bytes 3460
  723.4 133.5 %reduce-scatter.33.cloned.1.call-start = ((), (), s32[]{:S(2)}) async-start(), calls=%async_computation.31 | async-start | bytes 589824 | tf_op jit(solution)/shard_map/reduce_scatter | solution.py:394
  782.2 111.5 %reduce-scatter.31.cloned.1.call-start = ((), (), s32[]{:S(2)}) async-start(), calls=%async_computation.30 | async-start | bytes 4718592 | tf_op jit(solution)/shard_map/reduce_scatter | solution.py:393
  788.6 138.5 %reduce-scatter.27.cloned.1.call-start = ((), (), s32[]{:S(2)}) async-start(), calls=%async_computation.28 | async-start | bytes 1179648 | tf_op jit(solution)/shard_map/reduce_scatter | solution.py:391
  792.2 224.9 %reduce-scatter.29.cloned.1.call-start = ((), (), s32[]{:S(2)}) async-start(), calls=%async_computation.29 | async-start | bytes 9437184 | tf_op jit(solution)/shard_map/reduce_scatter | solution.py:392
  814.6 243.7 %reduce-scatter.25.cloned.1.call-start = ((), (), s32[]{:S(2)}) async-start(), calls=%async_computation.27 | async-start | bytes 3538944 | tf_op jit(solution)/shard_map/reduce_scatter | solution.py:390
  823.4 267.1 %reduce-scatter.21.cloned.1.call-start = ((), (), s32[]{:S(2)}) async-start(), calls=%async_computation.25 | async-start | bytes 294912 | tf_op jit(solution)/shard_map/reduce_scatter | solution.py:388
  824.5 27.9 %copy-start.80 = (f32[9,256]{1,0:T(8,128)S(1)}, f32[9,256]{1,0:T(8,128)}, u32[]{:S(2)}) copy-start(f32[9,256]{1,0:T(8,128)} %copy-done.79) | copy-start | bytes 27652
  824.5 27.9 %copy-start.131 = (bf16[9,128]{1,0:T(8,128)(2,1)S(1)}, bf16[9,128]{1,0:T(8,128)(2,1)}, u32[]{:S(2)}) copy-start(bf16[9,128]{1,0:T(8,128)(2,1)} %copy-done.130) | copy-start | bytes 6916
  824.5 27.9 %copy-start.133 = (bf16[9,128]{1,0:T(8,128)(2,1)S(1)}, bf16[9,128]{1,0:T(8,128)(2,1)}, u32[]{:S(2)}) copy-start(bf16[9,128]{1,0:T(8,128)(2,1)} %copy-done.132) | copy-start | bytes 6916
  856.8 276.8 %all-reduce.8.cloned.1.call-start = ((), (), s32[]{:S(2)}) async-start(), calls=%async_computation.33 | async-start | bytes 262144 | tf_op jit(solution)/shard_map/psum | solution.py:380
  857.6 368.1 %reduce-scatter.23.cloned.1.call-start = ((), (), s32[]{:S(2)}) async-start(), calls=%async_computation.26 | async-start | bytes 9437184 | tf_op jit(solution)/shard_map/reduce_scatter | solution.py:389
  864.7 407.4 %copy-start.33 = (f32[128,2,1024]{2,1,0:T(2,128)S(1)}, f32[128,2,1024]{2,1,0:T(2,128)}, u32[]{:S(2)}) copy-start(f32[128,2,1024]{2,1,0:T(2,128)} %param.43) | copy-start | bytes 3145732
  864.7 407.4 %copy-start.59 = (f32[128,2,1024]{2,1,0:T(2,128)S(1)}, f32[128,2,1024]{2,1,0:T(2,128)}, u32[]{:S(2)}) copy-start(f32[128,2,1024]{2,1,0:T(2,128)} %param.51) | copy-start | bytes 3145732
  1017.1 255.0 %copy-start.35 = (f32[128,2,1024]{2,0,1:T(8,128)S(1)}, f32[128,2,1024]{2,0,1:T(8,128)}, u32[]{:S(2)}) copy-start(f32[128,2,1024]{2,0,1:T(8,128)} %reduce-scatter.29.cloned.1.call-done) | copy-start | bytes 3145732
  (143 other events, 353.5 us)
Sparse Core Ops, SparseCore 0:
  10.2 49.8 all-gather.8
  64.2 42.1 all-reduce.5
  108.6 30.5 all-gather.12
  141.6 37.1 all-gather.10
  227.0 57.0 reduce-scatter.12
  286.2 47.1 all-gather.16
  336.0 36.1 all-gather.14
  374.4 30.8 all-gather.18
  412.5 56.1 reduce-scatter.14
  476.8 37.4 all-gather.20
  533.6 57.0 reduce-scatter.16
  599.0 37.4 all-gather.22
  720.5 57.0 reduce-scatter.18
  780.3 30.9 reduce-scatter.34
  814.0 29.1 reduce-scatter.32
  845.4 48.2 reduce-scatter.30
  896.5 30.5 reduce-scatter.26
  929.3 87.7 reduce-scatter.28
  1019.5 38.6 reduce-scatter.24
  1061.0 29.4 reduce-scatter.20
  1093.4 40.1 all-reduce.7
  1136.0 89.5 reduce-scatter.22
where the time goes:
time: 1310 us; the launch traced here: 1300 us
  waiting for transfers between devices  821 us (63%)
  matrix products  144 us (11%)
  blocking collectives  129 us (10%)
  other arithmetic  87.5 us (7%)
  local copies, waits for them, and re-layouts  85.8 us (7%)
  between operations  25.6 us (2%)
    reduce_scatter x1, waiting for transfers between devices, on_device(): lax.psum_scatter(grad_gateup, 'clip', scatter_dimension=0, tiled=True)  88.5 us
    reduce_scatter x1, waiting for transfers between devices, on_device(): lax.psum_scatter(grad_adapt, 'clip', scatter_dimension=1, tiled=True)  87.8 us
    reduce_scatter x1, waiting for transfers between devices, on_device(): lax.psum_scatter(two_part, 'row', scatter_dimension=2, tiled=True)  57.2 us
    reduce_scatter x1, waiting for transfers between devices, on_device(): lax.psum_scatter(one_part, 'row', scatter_dimension=2, tiled=True)  54.1 us
    reduce_scatter x1, waiting for transfers between devices, on_device(): lax.psum_scatter(branch_part, 'row', scatter_dimension=2, tiled=True)  53.5 us
    all_gather x1, waiting for transfers between devices, on_device(): lax.all_gather(w_gateup.astype(jnp.bfloat16), 'clip', axis=0, tiled=True)  45.1 us
    psum x1, waiting for transfers between devices, on_device(): lax.psum((adapt_rows, grad_patch, grad_head), 'row')  41.7 us
    all_gather x1, waiting for transfers between devices, on_device(): lax.all_gather(normed_one, 'row', axis=2, tiled=True)  39.6 us
  transfers between devices with their start and end apart: 22, of which 20 were waited for; matrix products, arithmetic and copies ran while one was open for 8% of the time, Pallas kernels for 0%

commit v1 on v0

v1 whole, which is shorter than its diff:
```python
import functools
import math
import types

import jax
import jax.numpy as jnp
import numpy as np
from jax import lax
from jax.experimental import pallas as pl
from jax.experimental.pallas import tpu as pltpu
from jax.sharding import PartitionSpec as P

D = 1024
HEADS = 16
HSIZE = 64
TF = 256
LEVELS = 1000
STEP = 3
VECTORS = 8
PAD = 16

norm_eps = 1e-06
clip_level = 0.002
learn_rate = 0.03
beta_one = 0.9
beta_two = 0.95
decay_rate = 0.1
adam_eps = 1e-08

MESH = pl.DeviceIdType.MESH
f32 = jnp.float32
bf16 = jnp.bfloat16


def dot_nn(left, right):
    return jnp.dot(left, right, preferred_element_type=f32)


def dot_nt(left, right):
    return lax.dot_general(left, right, (((1,), (1,)), ((), ())), preferred_element_type=f32)


def dot_tn(left, right):
    return lax.dot_general(left, right, (((0,), (0,)), ((), ())), preferred_element_type=f32)


def frequencies(number):
    return jnp.exp(-math.log(10000.0) * jnp.arange(number, dtype=f32) / number)


def noise_plan(levels):
    ratio = levels.astype(f32) / LEVELS
    alpha_bar = jnp.cos((ratio + 0.008) / 1.008 * (math.pi / 2)) ** 2
    weight = jnp.minimum(1.0, 5.0 * (1.0 - alpha_bar) / alpha_bar)
    return (alpha_bar, weight)


def level_embedding(levels, half):
    angle = levels.astype(f32)[..., None] * frequencies(half)
    return jnp.concatenate([jnp.cos(angle), jnp.sin(angle)], -1)


def sizes_of(latents, clips, parts):
    z = types.SimpleNamespace()
    z.C, z.R = clips, parts
    z.F = latents.shape[1]
    z.rows, z.cols, z.PF = latents.shape[2], latents.shape[3], latents.shape[4]
    z.LT = z.rows * z.cols
    z.N = 3 if z.F % 3 == 0 else 1
    z.CF = z.F // z.N
    z.CT = z.CF * z.LT
    z.W = z.R * z.CT
    z.T = z.F * z.LT
    z.HD = HEADS // parts
    z.HW = z.HD * HSIZE
    z.FH = 4 * D // parts
    z.DR = D // clips
    z.LR = TF // clips
    z.LW = D // parts
    z.AW = VECTORS * D // clips
    z.aw = z.AW // parts
    return z


def rotary_consts(z):
    half = HSIZE // 2
    fp = half // 4
    rp = 3 * half // 8
    cp = half - fp - rp

    def freq(n):
        return np.exp(-math.log(10000.0) * np.arange(n, dtype=np.float32) / np.float32(n)).astype(np.float32)

    shape = (z.N, z.R, z.CF, z.rows, z.cols)
    frame = (np.arange(z.N)[:, None] * z.CF + np.arange(z.CF)[None, :]).astype(np.float32)
    frame = np.broadcast_to(frame[:, None, :, None, None], shape)
    prow = (np.arange(z.R)[:, None] * z.rows + np.arange(z.rows)[None, :]).astype(np.float32)
    prow = np.broadcast_to(prow[None, :, None, :, None], shape)
    pcol = np.broadcast_to(np.arange(z.cols, dtype=np.float32), shape)
    angle = np.concatenate(
        [frame[..., None] * freq(fp), prow[..., None] * freq(rp), pcol[..., None] * freq(cp)], -1
    ).astype(np.float32)
    angle = angle.reshape(z.N, z.W, half)
    cos, sin = np.cos(angle), np.sin(angle)
    return np.concatenate([cos, cos, sin, sin], -1).astype(np.float32)


def remote(src, dst, send_sem, recv_sem, device):
    return pltpu.make_async_remote_copy(
        src_ref=src, dst_ref=dst, send_sem=send_sem, recv_sem=recv_sem, device_id=device, device_id_type=MESH
    )


def place(n, z):
    n.clip = lax.axis_index("clip")
    n.row = lax.axis_index("row")
    n.sib = n.clip + 1 - 2 * (n.clip % 2)
    n.row_peer = [(n.row + k) % z.R for k in range(1, z.R)]
    n.clip_peer = [(n.clip + k) % z.C for k in range(1, z.C)]
    n.square = z.R == 4
    n.far = (n.row + 1 - 2 * (n.row % 2) + 2) % z.R
    n.x = (n.clip, n.row + 1 - 2 * (n.row % 2))
    n.y = (n.clip, (n.row + 2) % z.R)
    n.arrivals = 2 if n.square else z.R - 1
    n.line = z.C == 8
    place = n.clip // 2
    n.inner = jnp.logical_or(place == 1, place == 2)
    n.far_end = jnp.where(n.inner, n.clip + 4 - 8 * (place // 2), n.clip)
    n.near_end = jnp.where(n.inner, n.clip - 2 + 4 * (place // 2), n.clip)
    n.core_peer = [(n.clip + 2 * k) % z.C for k in range(1, z.C // 2)]


def enter(n, z):
    barrier = pltpu.get_barrier_semaphore()
    for p in n.row_peer:
        pl.semaphore_signal(barrier, inc=1, device_id=(n.clip, p), device_id_type=MESH)
    for p in n.clip_peer:
        pl.semaphore_signal(barrier, inc=1, device_id=(p, n.row), device_id_type=MESH)
    pl.semaphore_wait(barrier, z.R + z.C - 2)


def send(src, dst, sems, slot, land, device):
    remote(src, dst, sems.at[(0,) + slot], sems.at[(1,) + land], device).start()


def sent(ref, sems, slot, device):
    remote(ref, ref, sems.at[(0,) + slot], sems.at[(1,) + slot], device).wait_send()


def got(ref, sems, slot, device):
    remote(ref, ref, sems.at[(0,) + slot], sems.at[(1,) + slot], device).wait_recv()


def halves(n, ref, c, p):
    rows = ref.shape[2] // 2
    return ref.at[c, p, :rows], ref.at[c, p, rows:]


def gather_row(n, full, sems, c):
    mine = full.at[c, n.row]
    if n.square:
        send(mine, mine, sems, (c, 0), (c, 0), n.x)
        send(mine, mine, sems, (c, 1), (c, 1), n.y)
        return
    for k, p in enumerate(n.row_peer):
        back = len(n.row_peer) - 1 - k
        send(mine, mine, sems, (c, k), (c, back), (n.clip, p))


def gather_more(n, full, sems, c):
    if n.square:
        got(full.at[c, n.x[1]], sems, (c, 0), n.x)
        block = halves(n, full, c, n.x[1])[0]
        send(block, block, sems, (c, 2), (c, 2), n.y)
        got(full.at[c, n.y[1]], sems, (c, 1), n.y)
        block = halves(n, full, c, n.y[1])[1]
        send(block, block, sems, (c, 3), (c, 3), n.x)


def gather_row_wait(n, full, sems, c):
    if n.square:
        low, high = halves(n, full, c, n.far)
        got(low, sems, (c, 2), n.y)
        got(high, sems, (c, 3), n.x)
        mine = full.at[c, n.row]
        sent(mine, sems, (c, 0), n.x)
        sent(mine, sems, (c, 1), n.y)
        sent(low, sems, (c, 2), n.y)
        sent(high, sems, (c, 3), n.x)
        return
    for k, p in enumerate(n.row_peer):
        block = full.at[c, p]
        got(block, sems, (c, k), (n.clip, p))
        sent(block, sems, (c, k), (n.clip, p))


def scatter_row(n, parts, landed, sems, c):
    if n.square:
        (xl, _), (_, yh), (fl, fh) = (halves(n, parts, c, p) for p in (n.x[1], n.y[1], n.far))
        send(fl, halves(n, landed, c, 2)[0], sems, (c, 0), (c, 0), n.x)
        send(fh, halves(n, landed, c, 2)[1], sems, (c, 1), (c, 1), n.y)
        send(xl, halves(n, landed, c, 0)[0], sems, (c, 2), (c, 2), n.x)
        send(yh, halves(n, landed, c, 1)[1], sems, (c, 3), (c, 3), n.y)
        return
    for k, p in enumerate(n.row_peer):
        back = len(n.row_peer) - 1 - k
        send(parts.at[c, p], landed.at[c, back], sems, (c, k), (c, back), (n.clip, p))


def scatter_more(n, parts, landed, sems, c):
    if n.square:
        rows = parts.shape[2] // 2
        low, high = halves(n, landed, c, 2)
        got(low, sems, (c, 0), n.x)
        parts[c, n.y[1], :rows] = (parts[c, n.y[1], :rows].astype(f32) + low[...].astype(f32)).astype(bf16)
        send(halves(n, parts, c, n.y[1])[0], halves(n, landed, c, 1)[0], sems, (c, 5), (c, 5), n.y)
        got(high, sems, (c, 1), n.y)
        parts[c, n.x[1], rows:] = (parts[c, n.x[1], rows:].astype(f32) + high[...].astype(f32)).astype(bf16)
        send(halves(n, parts, c, n.x[1])[1], halves(n, landed, c, 0)[1], sems, (c, 4), (c, 4), n.x)


def scatter_row_wait(n, parts, landed, sems, c):
    if n.square:
        (xl, xh), (yl, yh) = (halves(n, landed, c, k) for k in range(2))
        for slot, ref, peer in ((2, xl, n.x), (3, yh, n.y), (4, xh, n.x), (5, yl, n.y)):
            got(ref, sems, (c, slot), peer)
        for slot in range(6):
            sent(xl, sems, (c, slot), n.x)
        return
    for k, p in enumerate(n.row_peer):
        got(landed.at[c, k], sems, (c, k), (n.clip, p))
        sent(landed.at[c, k], sems, (c, k), (n.clip, p))


def share_row(n, buf, sems):
    for k, p in enumerate(n.row_peer):
        mine = buf.at[n.row]
        remote(mine, mine, sems.at[0, k], sems.at[1, n.row], (n.clip, p)).start()


def share_row_wait(n, buf, sems):
    for k, p in enumerate(n.row_peer):
        block = buf.at[p]
        remote(block, block, sems.at[0, k], sems.at[1, p], (n.clip, p)).wait()


def swap_row(n, src, dst, sems):
    for k, p in enumerate(n.row_peer):
        remote(src.at[p], dst.at[n.row], sems.at[0, k], sems.at[1, n.row], (n.clip, p)).start()


def swap_row_wait(n, src, dst, sems):
    for k, p in enumerate(n.row_peer):
        remote(src.at[p], dst.at[p], sems.at[0, k], sems.at[1, p], (n.clip, p)).wait()


def share_clip(n, buf, sems):
    for k, p in enumerate(n.clip_peer):
        mine = buf.at[n.clip]
        remote(mine, mine, sems.at[0, k], sems.at[1, n.clip], (p, n.row)).start()


def share_clip_wait(n, buf, sems):
    for k, p in enumerate(n.clip_peer):
        block = buf.at[p]
        remote(block, block, sems.at[0, k], sems.at[1, p], (p, n.row)).wait()


def swap_clip(n, src, dst, sems):
    for k, p in enumerate(n.clip_peer):
        remote(src.at[p], dst.at[n.clip], sems.at[0, k], sems.at[1, n.clip], (p, n.row)).start()


def swap_clip_wait(n, src, dst, sems):
    for k, p in enumerate(n.clip_peer):
        remote(src.at[p], dst.at[p], sems.at[0, k], sems.at[1, p], (p, n.row)).wait()


def skipped(n, z, p, relayed):
    if not relayed or not n.line:
        return None
    return jnp.logical_and(n.clip // 2 + p // 2 == 3, jnp.logical_not(n.inner))


def unless(skip, work):
    if skip is None:
        work()
    else:
        pl.when(jnp.logical_not(skip))(work)


def weight_send(n, z, buf, sems, relayed=False):
    mine = buf.at[n.clip]
    remote(mine, mine, sems.at[0, 0], sems.at[1, n.clip], (n.sib, n.row)).start()
    for k, p in enumerate(n.core_peer):
        copy = remote(mine, mine, sems.at[0, 1 + k], sems.at[1, n.clip], (p, n.row))
        unless(skipped(n, z, p, relayed), copy.start)


def weight_relay(n, z, buf, sems):
    if n.line:

        @pl.when(n.inner)
        def _():
            block = buf.at[n.far_end]
            remote(block, block, sems.at[0, 0], sems.at[1, n.far_end], (n.far_end, n.row)).wait_recv()
            remote(block, block, sems.at[0, z.C - 1], sems.at[1, n.far_end], (n.near_end, n.row)).start()


def weight_forward(n, z, buf, sems, relayed=False):
    for k, p in enumerate(n.core_peer):
        block = buf.at[p]
        known = jnp.logical_and(n.inner, p == n.far_end) if relayed and n.line else None
        unless(known, remote(block, block, sems.at[0, 1 + k], sems.at[1, p], (p, n.row)).wait_recv)
        remote(block, block, sems.at[0, z.C // 2 + k], sems.at[1, p], (n.sib, n.row)).start()


def weight_wait(n, z, buf, sems, relayed=False):
    block = buf.at[n.sib]
    remote(block, block, sems.at[0, 0], sems.at[1, n.sib], (n.sib, n.row)).wait()
    for k, p in enumerate(n.core_peer):
        j = (p // 2) * 2 + n.sib % 2
        block = buf.at[j]
        remote(block, block, sems.at[0, 1 + k], sems.at[1, j], (n.sib, n.row)).wait_recv()
        unless(skipped(n, z, p, relayed), remote(block, block, sems.at[0, 1 + k], sems.at[1, j], (n.sib, n.row)).wait_send)
        remote(block, block, sems.at[0, z.C // 2 + k], sems.at[1, j], (n.sib, n.row)).wait_send()
    if relayed and n.line:
        pl.when(n.inner)(remote(block, block, sems.at[0, z.C - 1], sems.at[1, n.sib], (n.sib, n.row)).wait_send)


def flat(x):
    return x.reshape((-1, x.shape[-1]))


def normed(x):
    centre = x - jnp.mean(x, -1, keepdims=True)
    rstd = lax.rsqrt(jnp.mean(centre * centre, -1, keepdims=True) + norm_eps)
    return centre * rstd, rstd


def norm_pull(n_hat, rstd, scale, grad):
    d_shift = jnp.sum(grad, 0, keepdims=True)
    d_scale = jnp.sum(grad * n_hat, 0, keepdims=True)
    dn = grad * (1.0 + scale)
    dx = rstd * (dn - jnp.mean(dn, -1, keepdims=True) - n_hat * jnp.mean(dn * n_hat, -1, keepdims=True))
    return dx, d_shift, d_scale


def vec(n, which, frame):
    return n.mod[which, pl.ds(frame, 1), :]


def frame_rows(z, c, i):
    return pl.ds(pl.multiple_of((c * z.CF + i) * z.LT, z.LT), z.LT)


def tables(n, c):
    x = n.tab[c]
    lane = lax.broadcasted_iota(jnp.int32, x.shape, 1)
    y = pltpu.roll(x, 64, 1)
    sin = jnp.where(lane < 64, y, x)
    return jnp.where(lane < 64, x, y), jnp.where(lane % HSIZE < HSIZE // 2, -sin, sin)


def turn(x, cos, sin):
    lane = lax.broadcasted_iota(jnp.int32, x.shape, 1)
    other = jnp.where(lane % HSIZE < HSIZE // 2, pltpu.roll(x, 128 - HSIZE // 2, 1), pltpu.roll(x, HSIZE // 2, 1))
    return x * cos + other * sin


def gelu_parts(x):
    k = math.sqrt(2.0 / math.pi)
    t = jnp.tanh(k * (x + 0.044715 * (x * x * x)))
    value = 0.5 * x * (1.0 + t)
    slope = 0.5 * (1.0 + t) + 0.5 * x * (1.0 - t * t) * (k * (1.0 + 3 * 0.044715 * (x * x)))
    return value, slope


def causal(z):
    a = (lax.broadcasted_iota(jnp.int32, (z.W, z.W), 0) % z.CT) // z.LT
    b = (lax.broadcasted_iota(jnp.int32, (z.W, z.W), 1) % z.CT) // z.LT
    return a, b


def after(z, c, more):
    if z.N > 1:
        pl.when(c > 0)(lambda: more(c - 1))


def last(z, c, more):
    if z.N > 1:
        pl.when(c == 0)(lambda: more(z.N - 1))


def phase_level(n, z):
    n.lv[n.clip] = n.w_level[...].astype(bf16)
    n.ea[n.clip] = n.emb[...]
    n.pt[n.clip] = n.w_patch[...]
    n.Wh[n.clip] = n.w_head[...].astype(bf16)
    enter(n, z)
    share_clip(n, n.ea, n.ea_s)
    share_clip(n, n.lv, n.lv_s)
    share_clip(n, n.pt, n.pt_s)
    for k in range(3):
        n.Wp[n.clip, :, k * z.HW : (k + 1) * z.HW] = n.wp[k].astype(bf16)
    n.Wo[n.clip] = jnp.transpose(n.wo[...]).astype(bf16)
    tiles = z.FH // 128
    for t in range(tiles):
        for k in range(2):
            at = k * z.FH + t * 128
            n.Wg[n.clip, :, at : at + 128] = n.wg[pl.ds(2 * t + k, z.DR, stride=2 * tiles), :].astype(bf16)
    n.Wd[n.clip] = jnp.transpose(n.wd[...]).astype(bf16)
    share_clip_wait(n, n.ea, n.ea_s)
    share_clip_wait(n, n.lv, n.lv_s)
    pre = dot_nn(flat(n.ea[...]), flat(n.lv[...]))
    n.pre[...] = pre
    cond = (pre * (1.0 / (1.0 + jnp.exp(-pre)))).astype(bf16)
    n.cond[...] = cond
    part = dot_nn(cond, n.w_adapt[...].astype(bf16))
    for p in range(z.R):
        n.pa[p] = part[:, p * z.aw : (p + 1) * z.aw]
    swap_row(n, n.pa, n.ra, n.ra_s)
    share_clip_wait(n, n.pt, n.pt_s)
    patch = flat(n.pt[...]).astype(bf16)
    for c in range(z.N):
        rows = slice(c * z.CT, (c + 1) * z.CT)
        n.stream[rows, :] = dot_nn(n.inputs[rows, :], patch)
    swap_row_wait(n, n.pa, n.ra, n.ra_s)
    total = n.pa[n.row]
    for p in n.row_peer:
        total = total + n.ra[p]
    n.rs[...] = total.reshape(z.C, PAD, z.aw)
    n.rb[n.clip] = n.rs[n.clip]
    swap_clip(n, n.rs, n.rb, n.rb_s)
    weight_send(n, z, n.Wp, n.Wp_s)
    swap_clip_wait(n, n.rs, n.rb, n.rb_s)
    n.ab[n.row] = n.rb[...]
    share_row(n, n.ab, n.ab_s)
    weight_send(n, z, n.Wo, n.Wo_s)
    share_clip(n, n.Wh, n.Wh_s)
    weight_send(n, z, n.Wg, n.Wg_s, True)
    weight_send(n, z, n.Wd, n.Wd_s)
    share_row_wait(n, n.ab, n.ab_s)
    for i in range(z.C):
        for r in range(z.R):
            col = i * z.AW + r * z.aw
            n.mod[col // D, :, col % D : col % D + z.aw] = n.ab[r, i]


def phase_one(n, z):
    def chunk(c, _):
        def frame(i, _):
            f = c * z.CF + i
            hat, unused = normed(n.stream[frame_rows(z, c, i), :])
            y = hat * (1.0 + vec(n, 1, f)) + vec(n, 0, f)
            n.one[c, n.row, pl.ds(pl.multiple_of(i * z.LT, z.LT), z.LT), :] = y.astype(bf16)
            return 0

        lax.fori_loop(0, z.CF, frame, 0)
        gather_row(n, n.one, n.one_s, c)
        after(z, c, lambda d: gather_more(n, n.one, n.one_s, d))
        return 0

    lax.fori_loop(0, z.N, chunk, 0)


def phase_attend(n, z):
    weight_forward(n, z, n.Wp, n.Wp_s)
    weight_wait(n, z, n.Wp, n.Wp_s)

    def chunk(c, _):
        if z.N == 1:
            gather_more(n, n.one, n.one_s, c)
        gather_row_wait(n, n.one, n.one_s, c)
        x = flat(n.one[c])
        pr = dot_nn(x, flat(n.Wp[...]))
        cos, sin = tables(n, c)
        for which in range(3):
            dest = (n.q, n.k, n.v)[which]
            for g in range(z.HW // 128):
                at = which * z.HW + g * 128
                y = pr[:, at : at + 128]
                if which < 2:
                    y = turn(y, cos, sin)
                if which == 0:
                    y = y * HSIZE**-0.5
                y = y.astype(bf16)
                for s in range(128 // HSIZE):
                    dest[g * (128 // HSIZE) + s, c] = y[:, s * HSIZE : (s + 1) * HSIZE]

        def head(h, _):
            q = n.q[h, c]
            a, b = causal(z)
            s = jnp.where(b <= a, dot_nt(q, n.k[h, c]), -1e30)
            m = jnp.max(s, -1, keepdims=True)
            e = jnp.exp(s - m)
            total = jnp.sum(e, -1, keepdims=True)
            o = dot_nn(e.astype(bf16), n.v[h, c])

            def more(j, carry):
                m, total, o = carry
                s = dot_nt(q, n.k[h, j])
                m2 = jnp.maximum(m, jnp.max(s, -1, keepdims=True))
                keep = jnp.exp(m - m2)
                e = jnp.exp(s - m2)
                total = total * keep + jnp.sum(e, -1, keepdims=True)
                o = o * keep + dot_nn(e.astype(bf16), n.v[h, j])
                return m2, total, o

            m, total, o = lax.fori_loop(0, c, more, (m, total, o))
            n.oh[h] = o / total
            lse = jnp.broadcast_to(m + jnp.log(total), (z.W, 128))
            n.lse[h, c] = jnp.transpose(lse)[:8]
            return 0

        lax.fori_loop(0, z.HD, head, 0)

        @pl.when(c == 0)
        def _():
            weight_forward(n, z, n.Wo, n.Wo_s)
            weight_wait(n, z, n.Wo, n.Wo_s)

        att = jnp.concatenate([n.oh[h] for h in range(z.HD)], -1)
        n.att[c] = att
        n.sb[c] = dot_nt(att.astype(bf16), flat(n.Wo[...])).astype(bf16).reshape(z.R, z.CT, D)
        last(z, c, lambda d: gather_more(n, n.one, n.one_s, d))
        scatter_row(n, n.sb, n.rsr, n.br_s, c)
        pl.when(c == (z.N - 1) // 2)(lambda: weight_relay(n, z, n.Wg, n.Wg_s))
        after(z, c, lambda d: scatter_more(n, n.sb, n.rsr, n.br_s, d))
        return 0

    lax.fori_loop(0, z.N, chunk, 0)


def summed(n, z, c, i):
    rows = pl.ds(pl.multiple_of(i * z.LT, z.LT), z.LT)
    total = n.sb[c, n.row, rows, :].astype(f32)
    for k in range(n.arrivals):
        total = total + n.rsr[c, k, rows, :].astype(f32)
    return total


def phase_two(n, z):
    def chunk(c, _):
        if z.N == 1:
            scatter_more(n, n.sb, n.rsr, n.br_s, c)
        scatter_row_wait(n, n.sb, n.rsr, n.br_s, c)

        def frame(i, _):
            f = c * z.CF + i
            rows = frame_rows(z, c, i)
            branch = summed(n, z, c, i)
            n.branch[rows, :] = branch
            mid = n.stream[rows, :] + vec(n, 2, f) * branch
            hat, unused = normed(mid)
            y = hat * (1.0 + vec(n, 4, f)) + vec(n, 3, f)
            n.two[c, n.row, pl.ds(pl.multiple_of(i * z.LT, z.LT), z.LT), :] = y.astype(bf16)
            return 0

        lax.fori_loop(0, z.CF, frame, 0)
        last(z, c, lambda d: scatter_more(n, n.sb, n.rsr, n.br_s, d))
        gather_row(n, n.two, n.two_s, c)
        after(z, c, lambda d: gather_more(n, n.two, n.two_s, d))
        return 0

    lax.fori_loop(0, z.N, chunk, 0)


def phase_feed(n, z):
    weight_forward(n, z, n.Wg, n.Wg_s, True)
    weight_wait(n, z, n.Wg, n.Wg_s, True)
    tile = 256

    def chunk(c, _):
        if z.N == 1:
            gather_more(n, n.two, n.two_s, c)
        gather_row_wait(n, n.two, n.two_s, c)

        def column(t, _):
            at = pl.ds(pl.multiple_of(t * tile, tile), tile)
            up_at = pl.ds(pl.multiple_of(z.FH + t * tile, tile), tile)
            x = flat(n.two[c])
            gate = dot_nn(x, flat(n.Wg[:, :, at]))
            up = dot_nn(x, flat(n.Wg[:, :, up_at]))
            value, unused = gelu_parts(gate)
            n.act[c, :, at] = (value * up).astype(bf16)
            n.gu[c, :, at] = gate.astype(bf16)
            n.gu[c, :, up_at] = up.astype(bf16)
            return 0

        lax.fori_loop(0, z.FH // tile, column, 0)

        @pl.when(c == 0)
        def _():
            weight_forward(n, z, n.Wd, n.Wd_s)
            weight_wait(n, z, n.Wd, n.Wd_s)

        slabs = tile // z.DR

        def output(t, _):
            y = dot_nt(n.act[c], flat(n.Wd[pl.ds(t * slabs, slabs)]))
            at = pl.ds(pl.multiple_of(t * tile, tile), tile)
            n.sb[c, :, :, at] = y.astype(bf16).reshape(z.R, z.CT, tile)
            return 0

        lax.fori_loop(0, D // tile, output, 0)
        last(z, c, lambda d: gather_more(n, n.two, n.two_s, d))
        scatter_row(n, n.sb, n.rsr, n.fd_s, c)
        after(z, c, lambda d: scatter_more(n, n.sb, n.rsr, n.fd_s, d))
        return 0

    lax.fori_loop(0, z.N, chunk, 0)


def phase_top(n, z):
    share_clip_wait(n, n.Wh, n.Wh_s)
    n.ghead[...] = jnp.zeros_like(n.ghead)
    n.loss[...] = jnp.zeros_like(n.loss)
    n.gad[...] = jnp.zeros_like(n.gad)

    def chunk(c, _):
        if z.N == 1:
            scatter_more(n, n.sb, n.rsr, n.fd_s, c)
        scatter_row_wait(n, n.sb, n.rsr, n.fd_s, c)

        def ahead(i, _):
            f = c * z.CF + i
            rows = frame_rows(z, c, i)
            here = pl.ds(pl.multiple_of(i * z.LT, z.LT), z.LT)
            feed = summed(n, z, c, i)
            mid = n.stream[rows, :] + vec(n, 2, f) * n.branch[rows, :]
            n.feed[here, :] = feed
            hat, rstd = normed(mid + vec(n, 5, f) * feed)
            n.hat[here, :] = hat
            n.rstd[here, :] = jnp.broadcast_to(rstd, (z.LT, 128))
            n.end[here, :] = (hat * (1.0 + vec(n, 7, f)) + vec(n, 6, f)).astype(bf16)
            return 0

        lax.fori_loop(0, z.CF, ahead, 0)
        rows = pl.ds(pl.multiple_of(c * z.CT, z.CT), z.CT)
        missed = dot_nn(n.end[...], flat(n.Wh[...])) - n.noise[rows, :]
        weight = n.fw[rows, :]
        n.loss[...] += jnp.sum((weight * (missed * missed)).reshape(z.CT // 8, 8, z.PF), 0)
        gp = ((2.0 / z.PF) * weight * missed).astype(bf16)
        n.ghead[...] += dot_tn(n.end[...], gp)
        n.gend[...] = dot_nt(gp, flat(n.Wh[...]))

        def back(i, _):
            f = c * z.CF + i
            rows = frame_rows(z, c, i)
            here = pl.ds(pl.multiple_of(i * z.LT, z.LT), z.LT)
            dx, d_shift, d_scale = norm_pull(n.hat[here, :], n.rstd[here, :1], vec(n, 7, f), n.gend[here, :])
            n.gad[6, pl.ds(f, 1), :] = d_shift
            n.gad[7, pl.ds(f, 1), :] = d_scale
            n.gad[5, pl.ds(f, 1), :] = jnp.sum(dx * n.feed[here, :], 0, keepdims=True)
            n.gmid[rows, :] = dx
            n.gf[c, n.row, here, :] = (dx * vec(n, 5, f)).astype(bf16)
            return 0

        lax.fori_loop(0, z.CF, back, 0)
        last(z, c, lambda d: scatter_more(n, n.sb, n.rsr, n.fd_s, d))
        gather_row(n, n.gf, n.gf_s, c)
        after(z, c, lambda d: gather_more(n, n.gf, n.gf_s, d))
        return 0

    lax.fori_loop(0, z.N, chunk, 0)


def run(body, z, cid, ins, anys, outs, scratch, export, vmem):
    names = list(ins) + list(anys) + list(outs) + list(scratch)

    def kernel(*refs):
        n = types.SimpleNamespace(**dict(zip(names, refs)))
        place(n, z)
        body(n, z)

    result = pl.pallas_call(
        kernel,
        out_shape=[jax.ShapeDtypeStruct(s, d) for s, d in outs.values()],
        in_specs=[pl.BlockSpec(memory_space=pltpu.VMEM)] * len(ins) + [pl.BlockSpec(memory_space=pl.ANY)] * len(anys),
        out_specs=[pl.BlockSpec(memory_space=pl.ANY if k in export else pltpu.VMEM) for k in outs],
        scratch_shapes=list(scratch.values()),
        compiler_params=pltpu.CompilerParams(collective_id=cid, has_side_effects=True, vmem_limit_bytes=vmem),
    )(*ins.values(), *anys.values())
    return dict(zip(outs, result))


KEPT = ("one", "two", "gf", "Wp", "Wo", "Wg", "Wd", "q", "k", "v", "att", "lse", "gu", "act", "stream", "branch", "gmid", "mod")


def forward_body(n, z):
    def export(*names):
        for name in names:
            i = KEPT.index(name)
            pltpu.make_async_copy(getattr(n, name), getattr(n, name + "_o"), n.ex_s.at[i]).start()

    phase_level(n, z)
    phase_one(n, z)
    export("mod", "stream")
    phase_attend(n, z)
    export("one", "Wp", "Wo", "q", "k", "v", "att", "lse")
    phase_two(n, z)
    export("branch")
    phase_feed(n, z)
    export("two", "Wg", "Wd", "gu", "act")
    phase_top(n, z)
    export("gmid")
    gather_more(n, n.gf, n.gf_s, z.N - 1)
    for c in range(z.N):
        gather_row_wait(n, n.gf, n.gf_s, c)
    export("gf")
    for i, name in enumerate(KEPT):
        pltpu.make_async_copy(getattr(n, name), getattr(n, name + "_o"), n.ex_s.at[i]).wait()


def shapes_of(z):
    rowed = (z.N, z.R, z.CT, D)
    return {
        "one": (rowed, bf16),
        "two": (rowed, bf16),
        "gf": (rowed, bf16),
        "gb": (rowed, bf16),
        "sb": (rowed, bf16),
        "rsr": ((z.N, z.R - 1, z.CT, D), bf16),
        "Wp": ((z.C, z.DR, 3 * z.HW), bf16),
        "Wo": ((z.C, z.DR, z.HW), bf16),
        "Wg": ((z.C, z.DR, 2 * z.FH), bf16),
        "Wd": ((z.C, z.DR, z.FH), bf16),
        "Wh": ((z.C, z.DR, z.PF), bf16),
        "q": ((z.HD, z.N, z.W, HSIZE), bf16),
        "k": ((z.HD, z.N, z.W, HSIZE), bf16),
        "v": ((z.HD, z.N, z.W, HSIZE), bf16),
        "att": ((z.N, z.W, z.HW), f32),
        "oh": ((z.HD, z.W, HSIZE), f32),
        "lse": ((z.HD, z.N, 8, z.W), f32),
        "gu": ((z.N, z.W, 2 * z.FH), bf16),
        "act": ((z.N, z.W, z.FH), bf16),
        "stream": ((z.T, D), f32),
        "branch": ((z.T, D), f32),
        "gmid": ((z.T, D), f32),
        "mod": ((VECTORS, PAD, D), f32),
        "gad": ((VECTORS, PAD, D), f32),
        "ghead": ((D, z.PF), f32),
        "loss": ((8, z.PF), f32),
        "pre": ((z.C * PAD, z.LW), f32),
        "cond": ((z.C * PAD, z.LW), bf16),
        "lv": ((z.C, z.LR, z.LW), bf16),
        "ea": ((z.C, PAD, TF), bf16),
        "pt": ((z.C, z.PF // z.C, D), f32),
        "pa": ((z.R, z.C * PAD, z.aw), f32),
        "ra": ((z.R, z.C * PAD, z.aw), f32),
        "rs": ((z.C, PAD, z.aw), f32),
        "rb": ((z.C, PAD, z.aw), f32),
        "ab": ((z.R, z.C, PAD, z.aw), f32),
        "feed": ((z.CT, D), f32),
        "hat": ((z.CT, D), f32),
        "rstd": ((z.CT, 128), f32),
        "end": ((z.CT, D), bf16),
        "gend": ((z.CT, D), f32),
    }


def vm(shapes, names):
    return {k: pltpu.VMEM(*shapes[k]) for k in names}


def forward_call(z, ins):
    sh = shapes_of(z)
    direct = ("gad", "ghead", "loss", "pre", "cond", "ea")
    outs = {k: sh[k] for k in direct}
    outs.update({k + "_o": sh[k] for k in KEPT})
    rest = ["Wh", "oh", "sb", "rsr", "lv", "pt", "pa", "ra", "rs", "rb", "ab", "feed", "hat", "rstd", "end", "gend"]
    scratch = vm(sh, list(KEPT) + rest)
    dma = pltpu.SemaphoreType.DMA
    for k in ("ea_s", "lv_s", "pt_s", "rb_s", "Wh_s", "Wp_s", "Wo_s", "Wg_s", "Wd_s"):
        scratch[k] = dma((2, z.C))
    for k in ("ra_s", "ab_s"):
        scratch[k] = dma((2, z.R))
    for k in ("one_s", "br_s", "two_s", "fd_s", "gf_s"):
        scratch[k] = dma((2, z.N, max(6, z.R)))
    scratch["ex_s"] = dma((len(KEPT),))
    got = run(forward_body, z, 0, ins, {}, outs, scratch, [k + "_o" for k in KEPT], 60 << 20)
    return {(k[:-2] if k.endswith("_o") else k): v for k, v in got.items()}


def forward_inputs(z, a):
    alpha_bar, frame_weight = noise_plan(a["levels"])
    latents = a["latents"].reshape(z.F, z.LT, z.PF)
    noise = a["noise"].reshape(z.F, z.LT, z.PF)
    noisy = jnp.sqrt(alpha_bar)[0, :, None, None] * latents + jnp.sqrt(1.0 - alpha_bar)[0, :, None, None] * noise
    emb = level_embedding(a["levels"][0], TF // 2).astype(bf16)
    return {
        "emb": jnp.pad(emb, ((0, PAD - z.F), (0, 0))),
        "w_level": a["w_level"],
        "w_patch": a["w_patch"],
        "w_head": a["w_head"],
        "w_adapt": a["w_adapt"],
        "wp": jnp.transpose(a["w_project"], (1, 0, 2)),
        "wo": a["w_output"],
        "wg": packed(a["w_gateup"]),
        "wd": a["w_down"],
        "inputs": noisy.astype(bf16).reshape(z.T, z.PF),
        "noise": noise.reshape(z.T, z.PF),
        "fw": jnp.broadcast_to(frame_weight[0][:, None, None], (z.F, z.LT, z.PF)).reshape(z.T, z.PF),
        "tab": jnp.asarray(rotary_consts(z)),
    }, frame_weight


def fetch(n, name):
    i = LOADED.index(name)
    return pltpu.make_async_copy(getattr(n, name + "_i"), getattr(n, name), n.in_s.at[i])


def phase_pull_feed(n, z):
    tile = 256
    for name in ("Wd", "gu", "gf"):
        fetch(n, name).wait()

    def chunk(c, _):
        def column(t, _):
            at = pl.ds(pl.multiple_of(t * tile, tile), tile)
            up_at = pl.ds(pl.multiple_of(z.FH + t * tile, tile), tile)
            da = dot_nn(flat(n.gf[c]), flat(n.Wd[:, :, at]))
            value, slope = gelu_parts(n.gu[c, :, at].astype(f32))
            up = n.gu[c, :, up_at].astype(f32)
            n.gu[c, :, at] = (da * up * slope).astype(bf16)
            n.gu[c, :, up_at] = (da * value).astype(bf16)
            return 0

        lax.fori_loop(0, z.FH // tile, column, 0)

        @pl.when(c == 0)
        def _():
            fetch(n, "Wg").wait()

        slabs = tile // z.DR

        def output(t, _):
            y = dot_nt(n.gu[c], flat(n.Wg[pl.ds(t * slabs, slabs)]))
            at = pl.ds(pl.multiple_of(t * tile, tile), tile)
            n.sb[c, :, :, at] = y.astype(bf16).reshape(z.R, z.CT, tile)
            return 0

        lax.fori_loop(0, D // tile, output, 0)
        scatter_row(n, n.sb, n.rsr, n.gt_s, c)
        after(z, c, lambda d: scatter_more(n, n.sb, n.rsr, n.gt_s, d))
        return 0

    lax.fori_loop(0, z.N, chunk, 0)


def weight_grad(n, z, left, right, into):
    half = n.tb.shape[0]
    width = right.shape[-1]
    tile = min(256, width)
    slabs = half // z.DR
    for part in range(D // half):
        for c in range(z.N):
            block = left[c, :, :, part * half : (part + 1) * half]
            n.tb[:, c * z.W : (c + 1) * z.W] = jnp.transpose(flat(block))

        def column(t, _):
            at = pl.ds(pl.multiple_of(t * tile, tile), tile)
            y = dot_nn(n.tb[...], flat(right[:, :, at]).astype(bf16))
            into[part * slabs : (part + 1) * slabs, :, at] = y.astype(bf16).reshape(slabs, z.DR, tile)
            return 0

        lax.fori_loop(0, width // tile, column, 0)


def reduce_one(n, z, part, sx, sems):
    for k in range(z.C // 2):
        j = (n.sib + 2 * k) % z.C
        remote(part.at[j], sx.at[j // 2], sems.at[0, k], sems.at[1, j // 2], (n.sib, n.row)).start()


def reduce_two(n, z, part, sx, sems, rx, more, width):
    for k in range(z.C // 2):
        j = (n.clip + 2 * k) % z.C
        mine = (n.sib + 2 * k) % z.C
        remote(part.at[mine], sx.at[j // 2], sems.at[0, k], sems.at[1, j // 2], (n.sib, n.row)).wait()
        part[j] = (part[j].astype(f32) + sx[j // 2].astype(f32)).astype(bf16)
        if k:
            back = z.C // 2 - k - 1
            at = slice(0, width)
            remote(part.at[j, :, at], rx.at[back, :, at], more.at[0, k], more.at[1, back], (j, n.row)).start()


def reduce_late(n, z):
    at = slice(2 * z.HW, 3 * z.HW)
    for k in range(1, z.C // 2):
        j = (n.clip + 2 * k) % z.C
        back = z.C // 2 - k - 1
        remote(n.Wp.at[j, :, at], n.Rp.at[back, :, at], n.Rv_s.at[0, k], n.Rv_s.at[1, back], (j, n.row)).start()


def reduce_three(n, z, part, rx, more, put, late):
    total = part[n.clip].astype(f32)
    for k in range(1, z.C // 2):
        j = (n.clip + 2 * k) % z.C
        at = slice(0, 2 * z.HW) if late else slice(0, part.shape[2])
        remote(part.at[j, :, at], rx.at[k - 1, :, at], more.at[0, k], more.at[1, k - 1], (j, n.row)).wait()
        if late:
            at = slice(2 * z.HW, 3 * z.HW)
            remote(part.at[j, :, at], rx.at[k - 1, :, at], n.Rv_s.at[0, k], n.Rv_s.at[1, k - 1], (j, n.row)).wait()
        total = total + rx[k - 1].astype(f32)
    put(total)
    n.squares[...] += fold(total)


def fold(x):
    x = x * x
    total = x[:, :128]
    for i in range(1, x.shape[1] // 128):
        total = total + x[:, i * 128 : (i + 1) * 128]
    return jnp.sum(total.reshape(x.shape[0] // 8, 8, 128), 0)


def phase_pull_two(n, z):
    for name in ("stream", "branch", "gmid"):
        fetch(n, name).wait()

    def chunk(c, _):
        scatter_row_wait(n, n.sb, n.rsr, n.gt_s, c)

        def frame(i, _):
            f = c * z.CF + i
            rows = frame_rows(z, c, i)
            branch = n.branch[rows, :]
            hat, rstd = normed(n.stream[rows, :] + vec(n, 2, f) * branch)
            dx, d_shift, d_scale = norm_pull(hat, rstd, vec(n, 4, f), summed(n, z, c, i))
            n.gadp[3, pl.ds(f, 1), :] = d_shift
            n.gadp[4, pl.ds(f, 1), :] = d_scale
            mid = n.gmid[rows, :] + dx
            n.gmid[rows, :] = mid
            n.gadp[2, pl.ds(f, 1), :] = jnp.sum(mid * branch, 0, keepdims=True)
            n.gb[c, n.row, pl.ds(pl.multiple_of(i * z.LT, z.LT), z.LT), :] = (mid * vec(n, 2, f)).astype(bf16)
            return 0

        lax.fori_loop(0, z.CF, frame, 0)
        gather_row(n, n.gb, n.gb_s, c)
        after(z, c, lambda d: gather_more(n, n.gb, n.gb_s, d))
        return 0

    lax.fori_loop(0, z.N, chunk, 0)


def phase_pull_attend(n, z):
    for name in ("Wo", "q", "k", "v", "att", "lse"):
        fetch(n, name).wait()
    queries = 384 if z.W % 384 == 0 else z.W
    parts = z.W // queries

    def chunk(c, _):
        if z.N == 1:
            gather_more(n, n.gb, n.gb_s, c)
        gather_row_wait(n, n.gb, n.gb_s, c)
        do = dot_nn(flat(n.gb[c]), flat(n.Wo[...])).astype(bf16)
        for h in range(z.HD):
            mine = do[:, h * HSIZE : (h + 1) * HSIZE]
            n.do[h] = mine
            delta = jnp.sum(mine.astype(f32) * n.att[c, :, h * HSIZE : (h + 1) * HSIZE], -1, keepdims=True)
            n.delta[h] = jnp.transpose(jnp.broadcast_to(delta, (z.W, 128)))[:8]

        def head(step, _):
            h, u = step // parts, step % parts
            at = pl.ds(pl.multiple_of(u * queries, queries), queries)
            q, do = n.q[h, c, at, :], n.do[h, at, :]
            lse, delta = n.lse[h, c, :, at][:1], n.delta[h, :, at][:1]

            def block(j, masked):
                k, v = n.k[h, j], n.v[h, j]
                p = jnp.exp(dot_nt(k, q) - lse)
                if masked:
                    a = lax.broadcasted_iota(jnp.int32, p.shape, 0)
                    b = lax.broadcasted_iota(jnp.int32, p.shape, 1) + u * queries
                    p = jnp.where((a % z.CT) // z.LT <= (b % z.CT) // z.LT, p, 0.0)
                dv = dot_nn(p.astype(bf16), do)
                ds = (p * (dot_nt(v, do) - delta)).astype(bf16)
                n.dkv[h, j] += jnp.concatenate([dot_nn(ds, q), dv], -1)
                return dot_tn(ds, k)

            dq = block(c, True)
            n.dq[h, at, :] = lax.fori_loop(0, c, lambda j, dq: dq + block(j, False), dq)
            return 0

        n.dkv[:, c] = jnp.zeros_like(n.dkv[:, c])
        lax.fori_loop(0, z.HD * parts, head, 0)
        last(z, c, lambda d: gather_more(n, n.gb, n.gb_s, d))
        pl.when(c == 0)(lambda: reduce_middle(n, z, "g"))
        pl.when(c == z.N // 2)(lambda: early_row(n, z))
        pl.when(c == z.N - 1)(lambda: early_clip(n, z))
        per = 128 // HSIZE
        cos, sin = tables(n, c)
        for g in range(z.HW // 128):
            y = jnp.concatenate([n.dq[g * per + s] for s in range(per)], -1)
            y = turn(y, cos, -sin) * HSIZE**-0.5
            n.gp[c, :, g * 128 : (g + 1) * 128] = y.astype(bf16)
        return 0

    lax.fori_loop(0, z.N, chunk, 0)


def phase_pull_project(n, z):
    fetch(n, "Wp").wait()
    per = 128 // HSIZE
    tile = 256

    def chunk(c, _):
        cos, sin = tables(n, c)
        for g in range(z.HW // 128):
            y = jnp.concatenate([n.dkv[g * per + s, c][:, :HSIZE] for s in range(per)], -1)
            n.gp[c, :, z.HW + g * 128 : z.HW + (g + 1) * 128] = turn(y, cos, -sin).astype(bf16)
            y = jnp.concatenate([n.dkv[g * per + s, c][:, HSIZE:] for s in range(per)], -1)
            n.gp[c, :, 2 * z.HW + g * 128 : 2 * z.HW + (g + 1) * 128] = y.astype(bf16)
        slabs = tile // z.DR

        def output(t, _):
            y = dot_nt(n.gp[c], flat(n.Wp[pl.ds(t * slabs, slabs)]))
            at = pl.ds(pl.multiple_of(t * tile, tile), tile)
            n.sb[c, :, :, at] = y.astype(bf16).reshape(z.R, z.CT, tile)
            return 0

        lax.fori_loop(0, D // tile, output, 0)
        scatter_row(n, n.sb, n.rsr, n.go_s, c)
        after(z, c, lambda d: scatter_more(n, n.sb, n.rsr, n.go_s, d))
        return 0

    lax.fori_loop(0, z.N, chunk, 0)


def phase_pull_one(n, z):
    def chunk(c, _):
        scatter_row_wait(n, n.sb, n.rsr, n.go_s, c)

        def frame(i, _):
            f = c * z.CF + i
            rows = frame_rows(z, c, i)
            hat, rstd = normed(n.stream[rows, :])
            dx, d_shift, d_scale = norm_pull(hat, rstd, vec(n, 1, f), summed(n, z, c, i))
            n.gadp[0, pl.ds(f, 1), :] = d_shift
            n.gadp[1, pl.ds(f, 1), :] = d_scale
            n.gb[c, n.row, pl.ds(pl.multiple_of(i * z.LT, z.LT), z.LT), :] = (n.gmid[rows, :] + dx).astype(bf16)
            return 0

        lax.fori_loop(0, z.CF, frame, 0)
        return 0

    lax.fori_loop(0, z.N, chunk, 0)


def row_total(n, src, dst, cut):
    total = src[n.row, cut].astype(f32)
    for p in n.row_peer:
        total = total + dst[p, cut].astype(f32)
    return total


def swap_row_cut(n, src, dst, sems, cut):
    for k, p in enumerate(n.row_peer):
        remote(src.at[p, cut], dst.at[n.row, cut], sems.at[0, k], sems.at[1, n.row], (n.clip, p)).start()


def swap_row_cut_wait(n, src, dst, sems, cut):
    for k, p in enumerate(n.row_peer):
        remote(src.at[p, cut], dst.at[p, cut], sems.at[0, k], sems.at[1, p], (n.clip, p)).wait()


def is_late(z, clip):
    return clip < z.C // 4


def swap_owner(n, z, late):
    for k, p in enumerate(n.clip_peer):
        copy = remote(n.ca.at[p], n.da.at[n.clip], n.ca_s.at[0, k], n.ca_s.at[1, n.clip], (p, n.row))
        pl.when(is_late(z, p) == late)(copy.start)


def swap_owner_wait(n, z):
    for k, p in enumerate(n.clip_peer):
        remote(n.ca.at[p], n.da.at[p], n.ca_s.at[0, k], n.ca_s.at[1, p], (p, n.row)).wait_recv()


def swap_owner_sent(n, z):
    for k, p in enumerate(n.clip_peer):
        remote(n.ca.at[p], n.da.at[p], n.ca_s.at[0, k], n.ca_s.at[1, p], (p, n.row)).wait_send()


def owner_share(n, z):
    swap_owner_wait(n, z)
    n.da[n.clip] = n.ca[n.clip]
    n.ea2[n.row] = flat(n.da[...])
    share_row(n, n.ea2, n.ea2_s)


def owner_grads(n, z):
    share_row_wait(n, n.ea2, n.ea2_s)
    low = jnp.concatenate([n.ea2[r] for r in range(z.R)], -1)
    n.gc[...] = dot_nt(low, n.w_adapt[...].astype(bf16)).reshape(z.C, PAD, z.LW)
    swap_clip(n, n.gc, n.gd, n.gc_s)
    gadapt = dot_tn(n.cond[...], low)
    n.gadapt[...] = gadapt
    n.squares[...] += fold(gadapt)


def take_columns(n, z, owners):
    for r in range(z.R):
        for i in owners:
            col = i * z.AW + r * z.aw
            n.xa[r, i] = n.gadp[col // D, :, col % D : col % D + z.aw]


def early_row(n, z):
    hr = z.DR // z.R
    take_columns(n, z, range(z.C // 4, z.C))
    for r in range(z.R):
        for i in range(z.C):
            at = i * z.DR + r * hr
            n.xh[r, i] = n.ghead[at : at + hr, :].astype(n.xh.dtype)
    swap_row_cut(n, n.xa, n.ya, n.xa_s, pl.ds(z.C // 4, z.C - z.C // 4))
    swap_row(n, n.xh, n.yh, n.xh_s)


def early_clip(n, z):
    cut = pl.ds(z.C // 4, z.C - z.C // 4)
    swap_row_cut_wait(n, n.xa, n.ya, n.xa_s, cut)
    swap_row_wait(n, n.xh, n.yh, n.xh_s)
    n.ca[cut] = row_total(n, n.xa, n.ya, cut).astype(bf16)
    n.ch[...] = row_total(n, n.xh, n.yh, slice(None)).astype(n.ch.dtype)
    swap_owner(n, z, False)
    swap_clip(n, n.ch, n.dh, n.ch_s)
    n.dh[n.clip] = n.ch[n.clip]


def phase_small(n, z):
    pr, hr = z.PF // z.C, z.DR // z.R
    pw = D // z.R
    late = is_late(z, n.clip)
    early = jnp.logical_not(late)
    cut = pl.ds(0, z.C // 4)
    take_columns(n, z, range(z.C // 4))
    swap_row_cut(n, n.xa, n.ya, n.xb_s, cut)
    gpatch = dot_tn(n.inputs[...], jnp.concatenate([n.gb[c, n.row] for c in range(z.N)], 0))
    for r in range(z.R):
        n.xp[r] = gpatch[:, r * pw : (r + 1) * pw].astype(bf16)
    swap_row(n, n.xp, n.yp, n.xp_s)
    pl.when(early)(lambda: owner_share(n, z))
    swap_clip_wait(n, n.ch, n.dh, n.ch_s)
    sh = n.dh[0].astype(f32)
    for i in range(1, z.C):
        sh = sh + n.dh[i].astype(f32)
    n.eh[n.row] = sh
    share_row(n, n.eh, n.eh_s)
    swap_row_cut_wait(n, n.xa, n.ya, n.xb_s, cut)
    n.ca[cut] = row_total(n, n.xa, n.ya, cut).astype(bf16)
    swap_owner(n, z, True)
    swap_row_wait(n, n.xp, n.yp, n.xp_s)
    n.cp[...] = row_total(n, n.xp, n.yp, slice(None)).reshape(z.C, pr, pw).astype(n.cp.dtype)
    swap_clip(n, n.cp, n.dp, n.cp_s)
    n.dp[n.clip] = n.cp[n.clip]
    pl.when(early)(lambda: owner_grads(n, z))
    reduce_late(n, z)
    pl.when(late)(lambda: owner_share(n, z))
    reduce_end(n, z, "d")
    pl.when(late)(lambda: owner_grads(n, z))
    swap_owner_sent(n, z)
    swap_clip_wait(n, n.cp, n.dp, n.cp_s)
    sp = n.dp[0].astype(f32)
    for i in range(1, z.C):
        sp = sp + n.dp[i].astype(f32)
    n.ep[n.row] = sp
    share_row(n, n.ep, n.ep_s)
    n.squares[...] += fold(sp) + fold(sh)
    reduce_end(n, z, "g")
    swap_clip_wait(n, n.gc, n.gd, n.gc_s)
    total = n.gc[n.clip]
    for p in n.clip_peer:
        total = total + n.gd[p]
    pre = n.pre[pl.ds(pl.multiple_of(n.clip * PAD, PAD), PAD), :]
    sig = 1.0 / (1.0 + jnp.exp(-pre))
    n.gl[n.clip] = (total * (sig * (1.0 + pre * (1.0 - sig)))).astype(bf16)
    share_clip(n, n.gl, n.gl_s)
    reduce_end(n, z, "o")
    reduce_end(n, z, "p")
    share_row_wait(n, n.eh, n.eh_s)
    share_row_wait(n, n.ep, n.ep_s)
    for r in range(z.R):
        n.gpatch[:, r * pw : (r + 1) * pw] = n.ep[r]
        n.gheads[r * hr : (r + 1) * hr, :] = n.eh[r]
    share_clip_wait(n, n.gl, n.gl_s)
    n.glv[...] = dot_tn(flat(n.ea[...]), flat(n.gl[...]))
    glevel = n.glv[pl.ds(pl.multiple_of(n.clip * z.LR, z.LR), z.LR), :]
    n.glevel[...] = glevel
    n.squares[...] += fold(glevel)


def phase_stats(n, z):
    n.sa[n.row, 0:8] = n.squares[...]
    n.sa[n.row, 8:16] = n.loss[...]
    n.sa[n.row, 16:24] = n.weight[...]
    share_row(n, n.sa, n.sa_s)
    share_row_wait(n, n.sa, n.sa_s)
    total = n.sa[0]
    for r in range(1, z.R):
        total = total + n.sa[r]
    n.sc[n.clip] = total
    share_clip(n, n.sc, n.sc_s)
    share_clip_wait(n, n.sc, n.sc_s)
    total = n.sc[0]
    for i in range(1, z.C):
        total = total + n.sc[i]
    n.stats[...] = total


LOADED = ("Wd", "gu", "gf", "Wg", "stream", "branch", "gmid", "act", "two", "Wo", "q", "k", "v", "att", "lse", "Wp", "one")


def reduce_start(n, z, x):
    reduce_one(n, z, getattr(n, "W" + x), getattr(n, "S" + x), getattr(n, "S" + x + "_s"))


def reduce_middle(n, z, x):
    part, rx = getattr(n, "W" + x), getattr(n, "R" + x)
    width = 2 * z.HW if x == "p" else part.shape[2]
    reduce_two(n, z, part, getattr(n, "S" + x), getattr(n, "S" + x + "_s"), rx, getattr(n, "R" + x + "_s"), width)


def reduce_end(n, z, x):
    def put(total):
        if x == "p":
            for k in range(3):
                n.Gp[k] = total[:, k * z.HW : (k + 1) * z.HW]
        elif x == "g":
            tiles = z.FH // 128
            for t in range(tiles):
                for k in range(2):
                    at = k * z.FH + t * 128
                    n.Gg[pl.ds(2 * t + k, z.DR, stride=2 * tiles), :] = total[:, at : at + 128]
        else:
            getattr(n, "G" + x)[...] = jnp.transpose(total)

    reduce_three(n, z, getattr(n, "W" + x), getattr(n, "R" + x), getattr(n, "R" + x + "_s"), put, x == "p")


def backward_body(n, z):
    for name in LOADED:
        if name not in ("one", "two"):
            fetch(n, name).start()
    n.squares[...] = jnp.zeros_like(n.squares)
    n.gadp[...] = n.gad[...]
    enter(n, z)
    phase_pull_feed(n, z)
    fetch(n, "act").wait()
    weight_grad(n, z, n.gf, n.act, n.Wd)
    load_two = pltpu.make_async_copy(n.two_i, n.gf, n.in_s.at[LOADED.index("two")])
    load_two.start()
    reduce_start(n, z, "d")
    scatter_more(n, n.sb, n.rsr, n.gt_s, z.N - 1)
    phase_pull_two(n, z)
    reduce_middle(n, z, "d")
    load_two.wait()
    weight_grad(n, z, n.gf, n.gu, n.Wg)
    load_one = pltpu.make_async_copy(n.one_i, n.gf, n.in_s.at[LOADED.index("one")])
    load_one.start()
    reduce_start(n, z, "g")
    phase_pull_attend(n, z)
    weight_grad(n, z, n.gb, n.att, n.Wo)
    reduce_start(n, z, "o")
    phase_pull_project(n, z)
    load_one.wait()
    reduce_middle(n, z, "o")
    weight_grad(n, z, n.gf, n.gp, n.Wp)
    reduce_start(n, z, "p")
    scatter_more(n, n.sb, n.rsr, n.go_s, z.N - 1)
    reduce_middle(n, z, "p")
    phase_pull_one(n, z)
    phase_small(n, z)
    phase_stats(n, z)


def backward_call(z, kept, ins):
    sh = shapes_of(z)
    pr, hr, pw = z.PF // z.C, z.DR // z.R, D // z.R
    head_type = f32 if hr % 16 else bf16
    patch_type = f32 if pr % 16 else bf16
    widths = {"p": 3 * z.HW, "o": z.HW, "g": 2 * z.FH, "d": z.FH}
    outs = {
        "Gp": ((3, z.DR, z.HW), f32),
        "Go": ((z.HW, z.DR), f32),
        "Gg": ((z.DR * 2 * z.FH // 128, 128), f32),
        "Gd": ((z.FH, z.DR), f32),
    }
    outs.update(
        gpatch=((pr, D), f32),
        gheads=((z.DR, z.PF), f32),
        gadapt=((z.LW, z.AW), f32),
        glevel=((z.LR, z.LW), f32),
        stats=((24, 128), f32),
    )
    anys = {k + "_i": kept[k] for k in LOADED}
    scratch = vm(sh, [k for k in LOADED if k not in ("one", "two")] + ["gb", "sb", "rsr"])
    for x, w in widths.items():
        scratch["S" + x] = pltpu.VMEM((z.C // 2, z.DR, w), bf16)
        scratch["R" + x] = pltpu.VMEM((z.C // 2 - 1, z.DR, w), bf16)
    extra = {
        "tb": ((D // max(2, z.W // 192), z.N * z.W), bf16),
        "do": ((z.HD, z.W, HSIZE), bf16),
        "delta": ((z.HD, 8, z.W), f32),
        "dq": ((z.HD, z.W, HSIZE), f32),
        "dkv": ((z.HD, z.N, z.W, 2 * HSIZE), f32),
        "gp": ((z.N, z.W, 3 * z.HW), bf16),
        "gadp": ((VECTORS, PAD, D), f32),
        "squares": ((8, 128), f32),
        "xa": ((z.R, z.C, PAD, z.aw), f32),
        "ya": ((z.R, z.C, PAD, z.aw), f32),
        "xp": ((z.R, z.PF, pw), bf16),
        "yp": ((z.R, z.PF, pw), bf16),
        "xh": ((z.R, z.C, hr, z.PF), head_type),
        "yh": ((z.R, z.C, hr, z.PF), head_type),
        "ca": ((z.C, PAD, z.aw), bf16),
        "da": ((z.C, PAD, z.aw), bf16),
        "cp": ((z.C, pr, pw), patch_type),
        "dp": ((z.C, pr, pw), patch_type),
        "ch": ((z.C, hr, z.PF), head_type),
        "dh": ((z.C, hr, z.PF), head_type),
        "ea2": ((z.R, z.C * PAD, z.aw), bf16),
        "ep": ((z.R, pr, pw), f32),
        "eh": ((z.R, hr, z.PF), f32),
        "gc": ((z.C, PAD, z.LW), f32),
        "gd": ((z.C, PAD, z.LW), f32),
        "gl": ((z.C, PAD, z.LW), bf16),
        "glv": ((TF, z.LW), f32),
        "sa": ((z.R, 24, 128), f32),
        "sc": ((z.C, 24, 128), f32),
    }
    scratch.update(vm(extra, extra))
    dma = pltpu.SemaphoreType.DMA
    scratch["Rv_s"] = dma((2, z.C // 2))
    scratch["in_s"] = dma((len(LOADED),))
    for x in widths:
        scratch["S" + x + "_s"] = dma((2, z.C // 2))
        scratch["R" + x + "_s"] = dma((2, z.C // 2))
    for k in ("gt_s", "gb_s", "go_s"):
        scratch[k] = dma((2, z.N, max(6, z.R)))
    for k in ("xa_s", "xb_s", "xp_s", "xh_s", "ea2_s", "ep_s", "eh_s", "sa_s"):
        scratch[k] = dma((2, z.R))
    for k in ("ca_s", "cp_s", "ch_s", "gc_s", "gl_s", "sc_s"):
        scratch[k] = dma((2, z.C))
    return run(backward_body, z, 1, ins, anys, outs, scratch, (), 64 << 20)


WEIGHTS = ("patch", "level", "adapt", "project", "output", "gateup", "down", "head")


def packed(x):
    rows, pair, width = x.shape
    return jnp.transpose(x.reshape(rows, pair, width // 128, 128), (0, 2, 1, 3)).reshape(-1, 128)


def unpacked(x, shape):
    rows, pair, width = shape
    return jnp.transpose(x.reshape(rows, width // 128, pair, 128), (0, 2, 1, 3)).reshape(shape)


def to_kernel(values):
    values = list(values)
    values[3] = jnp.transpose(values[3], (1, 0, 2))
    values[5] = packed(values[5])
    return values


def from_kernel(values, gateup_shape):
    values = list(values)
    values[3] = jnp.transpose(values[3], (1, 0, 2))
    values[5] = unpacked(values[5], gateup_shape)
    return values


def adam_kernel(pf, stats, *refs):
    grads, masters, firsts, seconds = (refs[8 * i : 8 * i + 8] for i in range(4))
    scalars = refs[32:35]
    news, means, squares = (refs[35 + 8 * i : 43 + 8 * i] for i in range(3))
    weight_sum = jnp.sum(stats[16:24])
    grad_norm = jnp.sqrt(jnp.full((8, 128), jnp.sum(stats[0:8]))) / weight_sum
    factor = jnp.minimum(1.0, clip_level / (grad_norm + 1e-06)) / weight_sum
    scalars[0][0, 0] = jnp.sum(stats[8:16]) / pf
    scalars[1][0, 0] = weight_sum
    scalars[2][0, 0] = jnp.max(grad_norm)
    factor = factor[:1, :1]
    for g, m, f, s, new, mean, square in zip(grads, masters, firsts, seconds, news, means, squares):
        grad = g[...] * factor
        first_new = beta_one * f[...] + (1.0 - beta_one) * grad
        second_new = beta_two * s[...] + (1.0 - beta_two) * grad * grad
        first_hat = first_new * (1.0 / (1.0 - beta_one**STEP))
        second_hat = second_new * (1.0 / (1.0 - beta_two**STEP))
        master = m[...]
        new[...] = master - learn_rate * (first_hat / (jnp.sqrt(second_hat) + adam_eps) + decay_rate * master)
        mean[...] = first_new
        square[...] = second_new


def adam_call(z, stats, grads, masters, firsts, seconds):
    steps = 4
    split = (None, None, 0, 1, 0, 0, 0, 0)

    def spec(x, axis):
        if axis is None:
            return pl.BlockSpec(x.shape, lambda i: (0,) * x.ndim)
        block = tuple(d // steps if k == axis else d for k, d in enumerate(x.shape))
        return pl.BlockSpec(block, lambda i: tuple(i if k == axis else 0 for k in range(x.ndim)))

    specs = [spec(x, axis) for x, axis in zip(masters, split)]
    shapes = [jax.ShapeDtypeStruct(x.shape, f32) for x in masters]
    scalar = jax.ShapeDtypeStruct((1, 1), f32)
    result = pl.pallas_call(
        functools.partial(adam_kernel, z.PF),
        grid=(steps,),
        out_shape=[scalar] * 3 + shapes * 3,
        in_specs=[pl.BlockSpec(stats.shape, lambda i: (0, 0))] + specs * 4,
        out_specs=[pl.BlockSpec((1, 1), lambda i: (0, 0), memory_space=pltpu.SMEM)] * 3 + specs * 3,
        compiler_params=pltpu.CompilerParams(vmem_limit_bytes=64 << 20),
    )(stats, *grads, *masters, *firsts, *seconds)
    return result[:3], result[3:11], result[11:19], result[19:27]


def on_device(latents, noise, levels, *weights):
    masters, firsts, seconds = weights[:8], weights[8:16], weights[16:]
    a = dict(zip(["w_" + k for k in WEIGHTS], masters))
    a.update(latents=latents, noise=noise, levels=levels)
    z = sizes_of(latents, lax.axis_size("clip"), lax.axis_size("row"))
    ins, frame_weight = forward_inputs(z, a)
    kept = forward_call(z, ins)
    weight = jnp.sum(frame_weight) * z.LT
    back = {k: kept[k] for k in ("gad", "ghead", "loss", "pre", "cond", "ea", "mod")}
    back.update({k: ins[k] for k in ("w_adapt", "inputs", "tab")})
    back["weight"] = jnp.zeros((8, 128), f32).at[0, 0].set(weight)
    g = backward_call(z, kept, back)
    grads = (g["gpatch"], g["glevel"], g["gadapt"], g["Gp"], g["Go"], g["Gg"], g["Gd"], g["gheads"])
    scalars, *results = adam_call(z, g["stats"], grads, *(to_kernel(x) for x in (masters, firsts, seconds)))
    results = [from_kernel(x, masters[5].shape) for x in results]
    return tuple(x.reshape(()) for x in scalars) + tuple(x for result in results for x in result)


def solution(mesh):
    tokens = P("clip", None, "row", None, None)
    by_clip = P("clip", None)
    weights = (by_clip, P("clip", "row"), P("row", "clip"), P("clip", None, "row"), P("row", "clip"))
    weights = weights + (P("clip", None, "row"), P("row", "clip"), by_clip)
    return jax.shard_map(
        on_device,
        mesh=mesh,
        in_specs=(tokens, tokens, by_clip) + weights * 3,
        out_specs=(P(), P(), P()) + weights * 3,
        check_vma=False,
    )
```

time: 1310 us -> 346 us (0.26)
  waiting for transfers between devices: 821 us -> 0 us
  Pallas kernels: 0 us -> 338 us
  matrix products: 144 us -> 0 us
  blocking collectives: 129 us -> 0 us
  local copies, waits for them, and re-layouts: 85.8 us -> 1.82 us
  other arithmetic: 87.5 us -> 4.49 us
  between operations: 25.6 us -> 1.51 us
    reduce_scatter x12 -> x0, waiting for transfers between devices: 510 us -> none  [the longest x1 88.5 us: on_device(): lax.psum_scatter(grad_gateup, 'clip', scatter_dimension=0, tiled=True)]
    pallas_call x0 -> x3, Pallas kernels: none -> 338 us  [the longest x2 327 us: run(): pl.pallas_call(kernel, out_shape=[jax.ShapeDtypeStruct(s, d) for s, d in...]
    all_gather x8 -> x0, waiting for transfers between devices: 244 us -> none  [the longest x1 45.1 us: on_device(): lax.all_gather(w_gateup.astype(jnp.bfloat16), 'clip', axis=0, tiled=True)]
    dot_general x42 -> x0, matrix products: 144 us -> none  [the longest x8 33.8 us: outer_product(): lax.dot_general(left, right, (((0,), (0,)), ((), ())), preferred_element_...]
    psum x2 -> x0, waiting for transfers between devices: 65.8 us -> none  [the longest x1 41.7 us: on_device(): lax.psum((adapt_rows, grad_patch, grad_head), 'row')]
    psum x2 -> x0, blocking collectives: 65.4 us -> none  [the longest x1 38.4 us: on_device(): lax.psum((loss_local, weight_local, squares_local), ('clip', 'row'))]
    all_gather x4 -> x0, blocking collectives: 63.7 us -> none  [the longest x1 18.5 us: on_device(): lax.all_gather(w_output.astype(jnp.bfloat16), 'clip', axis=1, tiled=True)]
    reduce_sum x27 -> x1, other arithmetic: 40 us -> 1.32 us  [on_device(): weight = jnp.sum(frame_weight) * z.LT]
  transfers between devices with their start and end apart: 22 -> 0, of which waited for: 20 -> 0; matrix products, arithmetic and copies ran while one was open for 8% -> 0% of each run, Pallas kernels for 0% -> 0%
where the time goes in v1:
time: 346 us; the launch traced here: 345 us
  Pallas kernels  338 us (98%)
  other arithmetic  4.49 us (1%)
    pallas_call x2, Pallas kernels, run(): pl.pallas_call(kernel, out_shape=[jax.ShapeDtypeStruct(s, d) for s, d in...  327 us
    pallas_call x1, Pallas kernels, adam_call(): pl.pallas_call(functools.partial(adam_kernel, z.PF), grid=(steps,), out_s...  11.2 us

profile of v1, /device:TPU:0, one launch (start us, length us, event | category | flops | bytes accessed | tf_op | source)
XLA Modules:
  0.0 345.5 jit_solution(12049604912691475097)
XLA Ops:
  0.7 0.7 convert_bitcast_fusion
  1.3 1.3 fusion.8
  3.3 0.6 scatter.4.refs_10_
  3.9 0.1 fusion.4
  4.0 0.6 fusion.6.refs_0_
  4.7 0.1 mul.63
  4.7 0.1 mul.64
  4.8 0.1 broadcast_in_dim.15
  4.9 0.1 broadcast_in_dim.16
  5.0 0.1 mul.68
  5.0 0.1 mul.69
  5.1 1.8 fusion.1.refs_9_.refs_8_
  6.9 0.8 broadcast_in_dim.17.refs_11_
  7.6 161.0 %shard_map.475 = (f32[8,16,1024]{2,1,0:T(8,128)}, f32[1024,128]{1,0:T(8,128)}, f32[8,128]{1,0:T(8,128)}, f32[128,256]{1,0:T(8,128)}, bf16[128,256]{1,0:T(8,128)(...) custom-call(bf16[16,256]{1,0:T(8,128)(2,1)} %fusion.6.refs_0_, ...), custom_call_target="tpu_custom_call" | custom-call | tf_op jit(solution)/shard_map/pallas_call | solution.py:677
  168.7 165.5 %shard_map.476 = (f32[3,128,256]{2,1,0:T(8,128)}, f32[256,128]{1,0:T(8,128)}, f32[2048,128]{1,0:T(8,128)}, f32[1024,128]{1,0:T(8,128)}, f32[16,1024]{1,0:T(8,128...) custom-call(f32[8,16,1024]{2,1,0:T(8,128)} %get-tuple-element.99.refs_0_, ...), custom_call_target="tpu_custom_call" | custom-call | tf_op jit(solution)/shard_map/pallas_call | solution.py:677
  334.2 11.2 %shard_map.477 = (f32[1,1]{1,0:T(1,128)}, f32[1,1]{1,0:T(1,128)}, f32[1,1]{1,0:T(1,128)}, f32[16,1024]{1,0:T(8,128)}, f32[32,256]{1,0:T(8,128)}, /*index=5*/f32[...) custom-call(f32[24,128]{1,0:T(8,128)} %get-tuple-element.123.stats, ...), custom_call_target="tpu_custom_call" | custom-call | tf_op jit(solution)/shard_map/pallas_call | solution.py:1415
  (2 shorter events, 0.0 us)

commit v2 on v1

--- a/solution.py
+++ b/solution.py
@@ -127,6 +127,7 @@
     n.inner = jnp.logical_or(place == 1, place == 2)
     n.far_end = jnp.where(n.inner, n.clip + 4 - 8 * (place // 2), n.clip)
     n.near_end = jnp.where(n.inner, n.clip - 2 + 4 * (place // 2), n.clip)
+    n.relay_to = jnp.where(place == 0, n.clip + 2, (n.clip - 2 + z.C) % z.C)
     n.core_peer = [(n.clip + 2 * k) % z.C for k in range(1, z.C // 2)]
 
 
@@ -395,15 +396,17 @@
 def phase_level(n, z):
     n.lv[n.clip] = n.w_level[...].astype(bf16)
     n.ea[n.clip] = n.emb[...]
-    n.pt[n.clip] = n.w_patch[...]
-    n.Wh[n.clip] = n.w_head[...].astype(bf16)
+    pw, hr = D // z.R, z.DR // z.R
+    n.pq[n.row, n.clip] = n.w_patch[:, pl.ds(pl.multiple_of(n.row * pw, pw), pw)].astype(n.pq.dtype)
+    n.hq[n.row, n.clip] = n.w_head[pl.ds(pl.multiple_of(n.row * hr, hr), hr), :].astype(n.hq.dtype)
     enter(n, z)
     share_clip(n, n.ea, n.ea_s)
     share_clip(n, n.lv, n.lv_s)
-    share_clip(n, n.pt, n.pt_s)
+    share_clip(n, n.pq.at[n.row], n.pq_s)
     for k in range(3):
         n.Wp[n.clip, :, k * z.HW : (k + 1) * z.HW] = n.wp[k].astype(bf16)
     n.Wo[n.clip] = jnp.transpose(n.wo[...]).astype(bf16)
+    weight_send(n, z, n.Wo, n.Wo_s)
     tiles = z.FH // 128
     for t in range(tiles):
         for k in range(2):
@@ -418,53 +421,71 @@
     n.cond[...] = cond
     part = dot_nn(cond, n.w_adapt[...].astype(bf16))
     for p in range(z.R):
-        n.pa[p] = part[:, p * z.aw : (p + 1) * z.aw]
+        for i in range(z.C):
+            block = part[i * PAD : i * PAD + z.F, p * z.aw : (p + 1) * z.aw]
+            n.pa[p, i * z.F : (i + 1) * z.F, :] = block
     swap_row(n, n.pa, n.ra, n.ra_s)
-    share_clip_wait(n, n.pt, n.pt_s)
-    patch = flat(n.pt[...]).astype(bf16)
-    for c in range(z.N):
-        rows = slice(c * z.CT, (c + 1) * z.CT)
-        n.stream[rows, :] = dot_nn(n.inputs[rows, :], patch)
+    share_clip_wait(n, n.pq.at[n.row], n.pq_s)
+    share_row(n, n.pq, n.pr_s)
     swap_row_wait(n, n.pa, n.ra, n.ra_s)
     total = n.pa[n.row]
     for p in n.row_peer:
         total = total + n.ra[p]
-    n.rs[...] = total.reshape(z.C, PAD, z.aw)
+    n.rs[...] = jnp.zeros_like(n.rs)
+    for i in range(z.C):
+        n.rs[i, : z.F, :] = total[i * z.F : (i + 1) * z.F]
     n.rb[n.clip] = n.rs[n.clip]
     swap_clip(n, n.rs, n.rb, n.rb_s)
     weight_send(n, z, n.Wp, n.Wp_s)
+    share_row_wait(n, n.pq, n.pr_s)
+    patch = jnp.concatenate([flat(n.pq[r]) for r in range(z.R)], -1).astype(bf16)
+    for c in range(z.N):
+        rows = slice(c * z.CT, (c + 1) * z.CT)
+        n.stream[rows, :] = dot_nn(n.inputs[rows, :], patch)
+    send_hat(n, z, 0)
     swap_clip_wait(n, n.rs, n.rb, n.rb_s)
-    n.ab[n.row] = n.rb[...]
+    for i in range(z.C):
+        n.ab[n.row, i * z.F : (i + 1) * z.F, :] = n.rb[i, : z.F, :]
     share_row(n, n.ab, n.ab_s)
-    weight_send(n, z, n.Wo, n.Wo_s)
-    share_clip(n, n.Wh, n.Wh_s)
+    share_clip(n, n.hq.at[n.row], n.hq_s)
     weight_send(n, z, n.Wg, n.Wg_s, True)
     weight_send(n, z, n.Wd, n.Wd_s)
+    for c in range(1, z.N):
+        send_hat(n, z, c)
+        gather_more(n, n.one, n.one_s, c - 1)
+    n.mod[...] = jnp.zeros_like(n.mod)
     share_row_wait(n, n.ab, n.ab_s)
     for i in range(z.C):
         for r in range(z.R):
             col = i * z.AW + r * z.aw
-            n.mod[col // D, :, col % D : col % D + z.aw] = n.ab[r, i]
-
-
-def phase_one(n, z):
-    def chunk(c, _):
-        def frame(i, _):
-            f = c * z.CF + i
-            hat, unused = normed(n.stream[frame_rows(z, c, i), :])
-            y = hat * (1.0 + vec(n, 1, f)) + vec(n, 0, f)
-            n.one[c, n.row, pl.ds(pl.multiple_of(i * z.LT, z.LT), z.LT), :] = y.astype(bf16)
-            return 0
-
-        lax.fori_loop(0, z.CF, frame, 0)
-        gather_row(n, n.one, n.one_s, c)
-        after(z, c, lambda d: gather_more(n, n.one, n.one_s, d))
+            n.mod[col // D, : z.F, col % D : col % D + z.aw] = n.ab[r, i * z.F : (i + 1) * z.F, :]
+
+
+def send_hat(n, z, c):
+    def frame(i, _):
+        hat, unused = normed(n.stream[frame_rows(z, c, i), :])
+        n.one[c, n.row, pl.ds(pl.multiple_of(i * z.LT, z.LT), z.LT), :] = hat.astype(bf16)
         return 0
 
-    lax.fori_loop(0, z.N, chunk, 0)
+    lax.fori_loop(0, z.CF, frame, 0)
+    gather_row(n, n.one, n.one_s, c)
+
+
+def modulate_chunk(n, z, c):
+    def frame(step, _):
+        p, i = step // z.CF, step % z.CF
+        f = c * z.CF + i
+        rows = pl.ds(pl.multiple_of(i * z.LT, z.LT), z.LT)
+        y = n.one[c, p, rows, :].astype(f32) * (1.0 + vec(n, 1, f)) + vec(n, 0, f)
+        n.one[c, p, rows, :] = y.astype(bf16)
+        return 0
+
+    lax.fori_loop(0, z.R * z.CF, frame, 0)
 
 
 def phase_attend(n, z):
+    queries = 384 if z.W % 384 == 0 else z.W
+    parts = z.W // queries
     weight_forward(n, z, n.Wp, n.Wp_s)
     weight_wait(n, z, n.Wp, n.Wp_s)
 
@@ -472,6 +493,7 @@
         if z.N == 1:
             gather_more(n, n.one, n.one_s, c)
         gather_row_wait(n, n.one, n.one_s, c)
+        modulate_chunk(n, z, c)
         x = flat(n.one[c])
         pr = dot_nn(x, flat(n.Wp[...]))
         cos, sin = tables(n, c)
@@ -488,32 +510,28 @@
                 for s in range(128 // HSIZE):
                     dest[g * (128 // HSIZE) + s, c] = y[:, s * HSIZE : (s + 1) * HSIZE]
 
-        def head(h, _):
-            q = n.q[h, c]
-            a, b = causal(z)
-            s = jnp.where(b <= a, dot_nt(q, n.k[h, c]), -1e30)
-            m = jnp.max(s, -1, keepdims=True)
-            e = jnp.exp(s - m)
-            total = jnp.sum(e, -1, keepdims=True)
-            o = dot_nn(e.astype(bf16), n.v[h, c])
-
-            def more(j, carry):
-                m, total, o = carry
-                s = dot_nt(q, n.k[h, j])
-                m2 = jnp.maximum(m, jnp.max(s, -1, keepdims=True))
-                keep = jnp.exp(m - m2)
-                e = jnp.exp(s - m2)
-                total = total * keep + jnp.sum(e, -1, keepdims=True)
-                o = o * keep + dot_nn(e.astype(bf16), n.v[h, j])
-                return m2, total, o
-
-            m, total, o = lax.fori_loop(0, c, more, (m, total, o))
-            n.oh[h] = o / total
-            lse = jnp.broadcast_to(m + jnp.log(total), (z.W, 128))
-            n.lse[h, c] = jnp.transpose(lse)[:8]
-            return 0
-
-        lax.fori_loop(0, z.HD, head, 0)
+        def heads(past):
+            def head(step, _):
+                h, u = step // parts, step % parts
+                at = pl.ds(pl.multiple_of(u * queries, queries), queries)
+                q = n.q[h, past, at, :]
+                s = dot_nt(q, n.k[h, past])
+                a = (lax.broadcasted_iota(jnp.int32, s.shape, 0) + u * queries) % z.CT // z.LT
+                b = lax.broadcasted_iota(jnp.int32, s.shape, 1) % z.CT // z.LT
+                scores = [dot_nt(q, n.k[h, j]) for j in range(past)] + [jnp.where(b <= a, s, -1e30)]
+                m = functools.reduce(jnp.maximum, [jnp.max(s, -1, keepdims=True) for s in scores])
+                exps = [jnp.exp(s - m) for s in scores]
+                total = sum(jnp.sum(e, -1, keepdims=True) for e in exps)
+                o = sum(dot_nn(e.astype(bf16), n.v[h, j]) for j, e in enumerate(exps))
+                n.oh[h, at, :] = o / total
+                lse = jnp.broadcast_to(m + jnp.log(total), (queries, 128))
+                n.lse[h, past, :, at] = jnp.transpose(lse)[:8]
+                return 0
+
+            lax.fori_loop(0, z.HD * parts, head, 0)
+
+        for past in range(z.N):
+            pl.when(c == past)(functools.partial(heads, past))
 
         @pl.when(c == 0)
         def _():
@@ -567,6 +585,8 @@
 
 
 def phase_feed(n, z):
+    share_clip_wait(n, n.hq.at[n.row], n.hq_s)
+    share_row(n, n.hq, n.hr_s)
     weight_forward(n, z, n.Wg, n.Wg_s, True)
     weight_wait(n, z, n.Wg, n.Wg_s, True)
     tile = 256
@@ -613,7 +633,11 @@
 
 
 def phase_top(n, z):
-    share_clip_wait(n, n.Wh, n.Wh_s)
+    share_row_wait(n, n.hq, n.hr_s)
+    hr = z.DR // z.R
+    for i in range(z.C):
+        for r in range(z.R):
+            n.Wh[i, r * hr : (r + 1) * hr, :] = n.hq[r, i].astype(bf16)
     n.ghead[...] = jnp.zeros_like(n.ghead)
     n.loss[...] = jnp.zeros_like(n.loss)
     n.gad[...] = jnp.zeros_like(n.gad)
@@ -695,7 +719,6 @@
             pltpu.make_async_copy(getattr(n, name), getattr(n, name + "_o"), n.ex_s.at[i]).start()
 
     phase_level(n, z)
-    phase_one(n, z)
     export("mod", "stream")
     phase_attend(n, z)
     export("one", "Wp", "Wo", "q", "k", "v", "att", "lse")
@@ -746,12 +769,13 @@
         "cond": ((z.C * PAD, z.LW), bf16),
         "lv": ((z.C, z.LR, z.LW), bf16),
         "ea": ((z.C, PAD, TF), bf16),
-        "pt": ((z.C, z.PF // z.C, D), f32),
-        "pa": ((z.R, z.C * PAD, z.aw), f32),
-        "ra": ((z.R, z.C * PAD, z.aw), f32),
+        "pq": ((z.R, z.C, z.PF // z.C, D // z.R), f32 if z.PF // z.C % 16 else bf16),
+        "hq": ((z.R, z.C, z.DR // z.R, z.PF), f32 if z.DR // z.R % 16 else bf16),
+        "pa": ((z.R, z.C * z.F, z.aw), f32),
+        "ra": ((z.R, z.C * z.F, z.aw), f32),
         "rs": ((z.C, PAD, z.aw), f32),
         "rb": ((z.C, PAD, z.aw), f32),
-        "ab": ((z.R, z.C, PAD, z.aw), f32),
+        "ab": ((z.R, z.C * z.F, z.aw), f32),
         "feed": ((z.CT, D), f32),
         "hat": ((z.CT, D), f32),
         "rstd": ((z.CT, 128), f32),
@@ -769,12 +793,12 @@
     direct = ("gad", "ghead", "loss", "pre", "cond", "ea")
     outs = {k: sh[k] for k in direct}
     outs.update({k + "_o": sh[k] for k in KEPT})
-    rest = ["Wh", "oh", "sb", "rsr", "lv", "pt", "pa", "ra", "rs", "rb", "ab", "feed", "hat", "rstd", "end", "gend"]
+    rest = ["Wh", "oh", "sb", "rsr", "lv", "pq", "hq", "pa", "ra", "rs", "rb", "ab", "feed", "hat", "rstd", "end", "gend"]
     scratch = vm(sh, list(KEPT) + rest)
     dma = pltpu.SemaphoreType.DMA
-    for k in ("ea_s", "lv_s", "pt_s", "rb_s", "Wh_s", "Wp_s", "Wo_s", "Wg_s", "Wd_s"):
+    for k in ("ea_s", "lv_s", "pq_s", "rb_s", "hq_s", "Wp_s", "Wo_s", "Wg_s", "Wd_s"):
         scratch[k] = dma((2, z.C))
-    for k in ("ra_s", "ab_s"):
+    for k in ("ra_s", "ab_s", "pr_s", "hr_s"):
         scratch[k] = dma((2, z.R))
     for k in ("one_s", "br_s", "two_s", "fd_s", "gf_s"):
         scratch[k] = dma((2, z.N, max(6, z.R)))
@@ -816,7 +840,8 @@
     for name in ("Wd", "gu", "gf"):
         fetch(n, name).wait()
 
-    def chunk(c, _):
+    def chunk(s, _):
+        c = z.N - 1 - s
         def column(t, _):
             at = pl.ds(pl.multiple_of(t * tile, tile), tile)
             up_at = pl.ds(pl.multiple_of(z.FH + t * tile, tile), tile)
@@ -829,7 +854,7 @@
 
         lax.fori_loop(0, z.FH // tile, column, 0)
 
-        @pl.when(c == 0)
+        @pl.when(s == 0)
         def _():
             fetch(n, "Wg").wait()
 
@@ -843,7 +868,7 @@
 
         lax.fori_loop(0, D // tile, output, 0)
         scatter_row(n, n.sb, n.rsr, n.gt_s, c)
-        after(z, c, lambda d: scatter_more(n, n.sb, n.rsr, n.gt_s, d))
+        after(z, s, lambda d: scatter_more(n, n.sb, n.rsr, n.gt_s, z.N - 1 - d))
         return 0
 
     lax.fori_loop(0, z.N, chunk, 0)
@@ -874,7 +899,7 @@
         remote(part.at[j], sx.at[j // 2], sems.at[0, k], sems.at[1, j // 2], (n.sib, n.row)).start()
 
 
-def reduce_two(n, z, part, sx, sems, rx, more, width):
+def reduce_two(n, z, part, sx, sems, rx, more, width, relayed):
     for k in range(z.C // 2):
         j = (n.clip + 2 * k) % z.C
         mine = (n.sib + 2 * k) % z.C
@@ -883,7 +908,26 @@
         if k:
             back = z.C // 2 - k - 1
             at = slice(0, width)
-            remote(part.at[j, :, at], rx.at[back, :, at], more.at[0, k], more.at[1, back], (j, n.row)).start()
+            copy = remote(part.at[j, :, at], rx.at[back, :, at], more.at[0, k], more.at[1, back], (j, n.row))
+            if relayed:
+                skip = skipped(n, z, j, True)
+                hold = jnp.logical_and(n.inner, k == 2)
+                pl.when(jnp.logical_not(jnp.logical_or(skip, hold)))(copy.start)
+                pl.when(skip)(remote(part.at[j], n.Xg, n.Xg_s.at[0], n.Xg_s.at[1], (n.relay_to, n.row)).start)
+            else:
+                copy.start()
+
+
+def reduce_relay(n, z):
+    if n.line:
+
+        @pl.when(n.inner)
+        def _():
+            j = (n.clip + 4) % z.C
+            remote(n.Wg.at[j], n.Xg, n.Xg_s.at[0], n.Xg_s.at[1], (j, n.row)).wait_recv()
+            n.Wg[j] = (n.Wg[j].astype(f32) + n.Xg[...].astype(f32)).astype(bf16)
+            back = z.C // 2 - 3
+            remote(n.Wg.at[j], n.Rg.at[back], n.Rg_s.at[0, 2], n.Rg_s.at[1, back], (j, n.row)).start()
 
 
 def reduce_late(n, z):
@@ -894,12 +938,16 @@
         remote(n.Wp.at[j, :, at], n.Rp.at[back, :, at], n.Rv_s.at[0, k], n.Rv_s.at[1, back], (j, n.row)).start()
 
 
-def reduce_three(n, z, part, rx, more, put, late):
+def reduce_three(n, z, part, rx, more, put, late, relayed):
     total = part[n.clip].astype(f32)
     for k in range(1, z.C // 2):
         j = (n.clip + 2 * k) % z.C
         at = slice(0, 2 * z.HW) if late else slice(0, part.shape[2])
-        remote(part.at[j, :, at], rx.at[k - 1, :, at], more.at[0, k], more.at[1, k - 1], (j, n.row)).wait()
+        copy = remote(part.at[j, :, at], rx.at[k - 1, :, at], more.at[0, k], more.at[1, k - 1], (j, n.row))
+        skip = skipped(n, z, j, relayed)
+        unless(skip, copy.wait)
+        if skip is not None:
+            pl.when(skip)(remote(part.at[j], n.Xg, n.Xg_s.at[0], n.Xg_s.at[1], (n.relay_to, n.row)).wait_send)
         if late:
             at = slice(2 * z.HW, 3 * z.HW)
             remote(part.at[j, :, at], rx.at[k - 1, :, at], n.Rv_s.at[0, k], n.Rv_s.at[1, k - 1], (j, n.row)).wait()
@@ -920,7 +968,8 @@
     for name in ("stream", "branch", "gmid"):
         fetch(n, name).wait()
 
-    def chunk(c, _):
+    def chunk(s, _):
+        c = z.N - 1 - s
         scatter_row_wait(n, n.sb, n.rsr, n.gt_s, c)
 
         def frame(i, _):
@@ -939,7 +988,8 @@
 
         lax.fori_loop(0, z.CF, frame, 0)
         gather_row(n, n.gb, n.gb_s, c)
-        after(z, c, lambda d: gather_more(n, n.gb, n.gb_s, d))
+        pl.when(s == 0)(lambda: reduce_middle(n, z, "d"))
+        after(z, s, lambda d: gather_more(n, n.gb, n.gb_s, z.N - 1 - d))
         return 0
 
     lax.fori_loop(0, z.N, chunk, 0)
@@ -948,10 +998,12 @@
 def phase_pull_attend(n, z):
     for name in ("Wo", "q", "k", "v", "att", "lse"):
         fetch(n, name).wait()
+    n.dkv[...] = jnp.zeros_like(n.dkv)
     queries = 384 if z.W % 384 == 0 else z.W
     parts = z.W // queries
 
-    def chunk(c, _):
+    def chunk(s, _):
+        c = z.N - 1 - s
         if z.N == 1:
             gather_more(n, n.gb, n.gb_s, c)
         gather_row_wait(n, n.gb, n.gb_s, c)
@@ -961,6 +1013,7 @@
             n.do[h] = mine
             delta = jnp.sum(mine.astype(f32) * n.att[c, :, h * HSIZE : (h + 1) * HSIZE], -1, keepdims=True)
             n.delta[h] = jnp.transpose(jnp.broadcast_to(delta, (z.W, 128)))[:8]
+        pl.when(s == 0)(lambda: reduce_middle(n, z, "g"))
 
         def head(step, _):
             h, u = step // parts, step % parts
@@ -984,53 +1037,51 @@
             n.dq[h, at, :] = lax.fori_loop(0, c, lambda j, dq: dq + block(j, False), dq)
             return 0
 
-        n.dkv[:, c] = jnp.zeros_like(n.dkv[:, c])
         lax.fori_loop(0, z.HD * parts, head, 0)
-        last(z, c, lambda d: gather_more(n, n.gb, n.gb_s, d))
-        pl.when(c == 0)(lambda: reduce_middle(n, z, "g"))
-        pl.when(c == z.N // 2)(lambda: early_row(n, z))
-        pl.when(c == z.N - 1)(lambda: early_clip(n, z))
+        last(z, s, lambda d: gather_more(n, n.gb, n.gb_s, z.N - 1 - d))
+        pl.when(s == z.N // 2)(lambda: early_row(n, z))
+        pl.when(s == z.N // 2)(lambda: reduce_relay(n, z))
+        pl.when(s == z.N - 1)(lambda: early_clip(n, z))
         per = 128 // HSIZE
         cos, sin = tables(n, c)
         for g in range(z.HW // 128):
             y = jnp.concatenate([n.dq[g * per + s] for s in range(per)], -1)
             y = turn(y, cos, -sin) * HSIZE**-0.5
             n.gp[c, :, g * 128 : (g + 1) * 128] = y.astype(bf16)
+        pl.when(s == 0)(fetch(n, "Wp").wait)
+        project_chunk(n, z, c)
+        after(z, s, lambda d: scatter_more(n, n.sb, n.rsr, n.go_s, z.N - 1 - d))
         return 0
 
     lax.fori_loop(0, z.N, chunk, 0)
 
 
-def phase_pull_project(n, z):
-    fetch(n, "Wp").wait()
+def project_chunk(n, z, c):
     per = 128 // HSIZE
     tile = 256
-
-    def chunk(c, _):
-        cos, sin = tables(n, c)
-        for g in range(z.HW // 128):
-            y = jnp.concatenate([n.dkv[g * per + s, c][:, :HSIZE] for s in range(per)], -1)
-            n.gp[c, :, z.HW + g * 128 : z.HW + (g + 1) * 128] = turn(y, cos, -sin).astype(bf16)
-            y = jnp.concatenate([n.dkv[g * per + s, c][:, HSIZE:] for s in range(per)], -1)
-            n.gp[c, :, 2 * z.HW + g * 128 : 2 * z.HW + (g + 1) * 128] = y.astype(bf16)
-        slabs = tile // z.DR
-
-        def output(t, _):
-            y = dot_nt(n.gp[c], flat(n.Wp[pl.ds(t * slabs, slabs)]))
-            at = pl.ds(pl.multiple_of(t * tile, tile), tile)
-            n.sb[c, :, :, at] = y.astype(bf16).reshape(z.R, z.CT, tile)
-            return 0
-
-        lax.fori_loop(0, D // tile, output, 0)
-        scatter_row(n, n.sb, n.rsr, n.go_s, c)
-        after(z, c, lambda d: scatter_more(n, n.sb, n.rsr, n.go_s, d))
+    slabs = tile // z.DR
+    cos, sin = tables(n, c)
+    for g in range(z.HW // 128):
+        at = z.HW + g * 128
+        y = jnp.concatenate([n.dkv[g * per + h, c][:, :HSIZE] for h in range(per)], -1)
+        n.gp[c, :, at : at + 128] = turn(y, cos, -sin).astype(bf16)
+        at = 2 * z.HW + g * 128
+        y = jnp.concatenate([n.dkv[g * per + h, c][:, HSIZE:] for h in range(per)], -1)
+        n.gp[c, :, at : at + 128] = y.astype(bf16)
+
+    def output(t, _):
+        y = dot_nt(n.gp[c], flat(n.Wp[pl.ds(t * slabs, slabs)]))
+        at = pl.ds(pl.multiple_of(t * tile, tile), tile)
+        n.sb[c, :, :, at] = y.astype(bf16).reshape(z.R, z.CT, tile)
         return 0
 
-    lax.fori_loop(0, z.N, chunk, 0)
+    lax.fori_loop(0, D // tile, output, 0)
+    scatter_row(n, n.sb, n.rsr, n.go_s, c)
 
 
 def phase_pull_one(n, z):
-    def chunk(c, _):
+    def chunk(s, _):
+        c = z.N - 1 - s
         scatter_row_wait(n, n.sb, n.rsr, n.go_s, c)
 
         def frame(i, _):
@@ -1195,9 +1246,8 @@
 
 
 def phase_stats(n, z):
-    n.sa[n.row, 0:8] = n.squares[...]
-    n.sa[n.row, 8:16] = n.loss[...]
-    n.sa[n.row, 16:24] = n.weight[...]
+    lines = [jnp.sum(ref[...], 0, keepdims=True) for ref in (n.squares, n.loss, n.weight)]
+    n.sa[n.row] = jnp.concatenate(lines + [jnp.zeros((5, 128), f32)], 0)
     share_row(n, n.sa, n.sa_s)
     share_row_wait(n, n.sa, n.sa_s)
     total = n.sa[0]
@@ -1222,7 +1272,7 @@
 def reduce_middle(n, z, x):
     part, rx = getattr(n, "W" + x), getattr(n, "R" + x)
     width = 2 * z.HW if x == "p" else part.shape[2]
-    reduce_two(n, z, part, getattr(n, "S" + x), getattr(n, "S" + x + "_s"), rx, getattr(n, "R" + x + "_s"), width)
+    reduce_two(n, z, part, getattr(n, "S" + x), getattr(n, "S" + x + "_s"), rx, getattr(n, "R" + x + "_s"), width, x == "g" and n.line)
 
 
 def reduce_end(n, z, x):
@@ -1239,7 +1289,7 @@
         else:
             getattr(n, "G" + x)[...] = jnp.transpose(total)
 
-    reduce_three(n, z, getattr(n, "W" + x), getattr(n, "R" + x), getattr(n, "R" + x + "_s"), put, x == "p")
+    reduce_three(n, z, getattr(n, "W" + x), getattr(n, "R" + x), getattr(n, "R" + x + "_s"), put, x == "p", x == "g")
 
 
 def backward_body(n, z):
@@ -1248,6 +1298,13 @@
             fetch(n, name).start()
     n.squares[...] = jnp.zeros_like(n.squares)
     n.gadp[...] = n.gad[...]
+    if n.line:
+        for k, p in enumerate(n.core_peer):
+
+            @pl.when(skipped(n, z, p, True))
+            def _():
+                n.Rg[k] = jnp.zeros_like(n.Rg[k])
+
     enter(n, z)
     phase_pull_feed(n, z)
     fetch(n, "act").wait()
@@ -1255,24 +1312,22 @@
     load_two = pltpu.make_async_copy(n.two_i, n.gf, n.in_s.at[LOADED.index("two")])
     load_two.start()
     reduce_start(n, z, "d")
-    scatter_more(n, n.sb, n.rsr, n.gt_s, z.N - 1)
+    scatter_more(n, n.sb, n.rsr, n.gt_s, 0)
     phase_pull_two(n, z)
-    reduce_middle(n, z, "d")
     load_two.wait()
     weight_grad(n, z, n.gf, n.gu, n.Wg)
     load_one = pltpu.make_async_copy(n.one_i, n.gf, n.in_s.at[LOADED.index("one")])
     load_one.start()
     reduce_start(n, z, "g")
     phase_pull_attend(n, z)
+    load_one.wait()
+    weight_grad(n, z, n.gf, n.gp, n.Wp)
+    scatter_more(n, n.sb, n.rsr, n.go_s, 0)
+    reduce_start(n, z, "p")
     weight_grad(n, z, n.gb, n.att, n.Wo)
     reduce_start(n, z, "o")
-    phase_pull_project(n, z)
-    load_one.wait()
+    reduce_middle(n, z, "p")
     reduce_middle(n, z, "o")
-    weight_grad(n, z, n.gf, n.gp, n.Wp)
-    reduce_start(n, z, "p")
-    scatter_more(n, n.sb, n.rsr, n.go_s, z.N - 1)
-    reduce_middle(n, z, "p")
     phase_pull_one(n, z)
     phase_small(n, z)
     phase_stats(n, z)
@@ -1295,7 +1350,7 @@
         gheads=((z.DR, z.PF), f32),
         gadapt=((z.LW, z.AW), f32),
         glevel=((z.LR, z.LW), f32),
-        stats=((24, 128), f32),
+        stats=((8, 128), f32),
     )
     anys = {k + "_i": kept[k] for k in LOADED}
     scratch = vm(sh, [k for k in LOADED if k not in ("one", "two")] + ["gb", "sb", "rsr"])
@@ -1330,11 +1385,14 @@
         "gd": ((z.C, PAD, z.LW), f32),
         "gl": ((z.C, PAD, z.LW), bf16),
         "glv": ((TF, z.LW), f32),
-        "sa": ((z.R, 24, 128), f32),
-        "sc": ((z.C, 24, 128), f32),
+        "sa": ((z.R, 8, 128), f32),
+        "sc": ((z.C, 8, 128), f32),
     }
     scratch.update(vm(extra, extra))
     dma = pltpu.SemaphoreType.DMA
+    if z.C == 8:
+        scratch["Xg"] = pltpu.VMEM((z.DR, 2 * z.FH), bf16)
+        scratch["Xg_s"] = dma((2,))
     scratch["Rv_s"] = dma((2, z.C // 2))
     scratch["in_s"] = dma((len(LOADED),))
     for x in widths:
@@ -1380,10 +1438,10 @@
     grads, masters, firsts, seconds = (refs[8 * i : 8 * i + 8] for i in range(4))
     scalars = refs[32:35]
     news, means, squares = (refs[35 + 8 * i : 43 + 8 * i] for i in range(3))
-    weight_sum = jnp.sum(stats[16:24])
-    grad_norm = jnp.sqrt(jnp.full((8, 128), jnp.sum(stats[0:8]))) / weight_sum
+    weight_sum = jnp.sum(stats[2:3])
+    grad_norm = jnp.sqrt(jnp.full((8, 128), jnp.sum(stats[0:1]))) / weight_sum
     factor = jnp.minimum(1.0, clip_level / (grad_norm + 1e-06)) / weight_sum
-    scalars[0][0, 0] = jnp.sum(stats[8:16]) / pf
+    scalars[0][0, 0] = jnp.sum(stats[1:2]) / pf
     scalars[1][0, 0] = weight_sum
     scalars[2][0, 0] = jnp.max(grad_norm)
     factor = factor[:1, :1]

time: 346 us -> 315 us (0.910)
  Pallas kernels: 338 us -> 307 us
    pallas_call x2, Pallas kernels: 327 us -> 296 us  [run(): pl.pallas_call(kernel, out_shape=[jax.ShapeDtypeStruct(s, d) for s, d in...]
where the time goes in v2:
time: 315 us
  Pallas kernels  307 us (97%)
  other arithmetic  4.49 us (1%)
    pallas_call x2, Pallas kernels, run(): pl.pallas_call(kernel, out_shape=[jax.ShapeDtypeStruct(s, d) for s, d in...  296 us
    pallas_call x1, Pallas kernels, adam_call(): pl.pallas_call(functools.partial(adam_kernel, z.PF), grid=(steps,), out_s...  11.2 us

profile of v2, /device:TPU:0, one launch (start us, length us, event | category | flops | bytes accessed | tf_op | source)
XLA Modules:
  0.0 314.7 jit_solution(4802601888509104073)
XLA Ops:
  0.7 0.7 convert_bitcast_fusion
  1.3 1.3 fusion.8
  3.3 0.6 scatter.4.refs_10_
  3.9 0.1 fusion.4
  4.0 0.6 fusion.6.refs_0_
  4.7 0.1 mul.63
  4.7 0.1 mul.64
  4.8 0.1 broadcast_in_dim.15
  4.9 0.1 broadcast_in_dim.16
  5.0 0.1 mul.68
  5.0 0.1 mul.69
  5.1 1.8 fusion.1.refs_9_.refs_8_
  6.9 0.8 broadcast_in_dim.17.refs_11_
  7.6 147.7 %shard_map.475 = (f32[8,16,1024]{2,1,0:T(8,128)}, f32[1024,128]{1,0:T(8,128)}, f32[8,128]{1,0:T(8,128)}, f32[128,256]{1,0:T(8,128)}, bf16[128,256]{1,0:T(8,128)(...) custom-call(bf16[16,256]{1,0:T(8,128)(2,1)} %fusion.6.refs_0_, ...), custom_call_target="tpu_custom_call" | custom-call | tf_op jit(solution)/shard_map/pallas_call | solution.py:701
  155.4 147.9 %shard_map.476 = (f32[3,128,256]{2,1,0:T(8,128)}, f32[256,128]{1,0:T(8,128)}, f32[2048,128]{1,0:T(8,128)}, f32[1024,128]{1,0:T(8,128)}, f32[16,1024]{1,0:T(8,128...) custom-call(f32[8,16,1024]{2,1,0:T(8,128)} %get-tuple-element.99.refs_0_, ...), custom_call_target="tpu_custom_call" | custom-call | tf_op jit(solution)/shard_map/pallas_call | solution.py:701
  303.3 11.2 %shard_map.477 = (f32[1,1]{1,0:T(1,128)}, f32[1,1]{1,0:T(1,128)}, f32[1,1]{1,0:T(1,128)}, f32[16,1024]{1,0:T(8,128)}, f32[32,256]{1,0:T(8,128)}, /*index=5*/f32[...) custom-call(f32[8,128]{1,0:T(8,128)} %get-tuple-element.123.stats, ...), custom_call_target="tpu_custom_call" | custom-call | tf_op jit(solution)/shard_map/pallas_call | solution.py:1473
  (2 shorter events, 0.0 us)

commit v3 on v2

--- a/solution.py
+++ b/solution.py
@@ -394,6 +394,8 @@
 
 
 def phase_level(n, z):
+    for name in HELD:
+        hold(n, name).start()
     n.lv[n.clip] = n.w_level[...].astype(bf16)
     n.ea[n.clip] = n.emb[...]
     pw, hr = D // z.R, z.DR // z.R
@@ -403,6 +405,8 @@
     share_clip(n, n.ea, n.ea_s)
     share_clip(n, n.lv, n.lv_s)
     share_clip(n, n.pq.at[n.row], n.pq_s)
+    for name in ("wp", "wo", "wg", "wd"):
+        hold(n, name).wait()
     for k in range(3):
         n.Wp[n.clip, :, k * z.HW : (k + 1) * z.HW] = n.wp[k].astype(bf16)
     n.Wo[n.clip] = jnp.transpose(n.wo[...]).astype(bf16)
@@ -419,6 +423,7 @@
     n.pre[...] = pre
     cond = (pre * (1.0 / (1.0 + jnp.exp(-pre)))).astype(bf16)
     n.cond[...] = cond
+    hold(n, "w_adapt").wait()
     part = dot_nn(cond, n.w_adapt[...].astype(bf16))
     for p in range(z.R):
         for i in range(z.C):
@@ -438,6 +443,8 @@
     swap_clip(n, n.rs, n.rb, n.rb_s)
     weight_send(n, z, n.Wp, n.Wp_s)
     share_row_wait(n, n.pq, n.pr_s)
+    for name in ("inputs", "tab", "noise", "fw"):
+        hold(n, name).wait()
     patch = jnp.concatenate([flat(n.pq[r]) for r in range(z.R)], -1).astype(bf16)
     for c in range(z.N):
         rows = slice(c * z.CT, (c + 1) * z.CT)
@@ -640,6 +647,7 @@
             n.Wh[i, r * hr : (r + 1) * hr, :] = n.hq[r, i].astype(bf16)
     n.ghead[...] = jnp.zeros_like(n.ghead)
     n.loss[...] = jnp.zeros_like(n.loss)
+    n.weight[...] = jnp.sum(n.fw[...].reshape(z.T // 8, 8, z.PF), 0) * (1.0 / z.PF)
     n.gad[...] = jnp.zeros_like(n.gad)
 
     def chunk(c, _):
@@ -710,6 +718,13 @@
 
 
 KEPT = ("one", "two", "gf", "Wp", "Wo", "Wg", "Wd", "q", "k", "v", "att", "lse", "gu", "act", "stream", "branch", "gmid", "mod")
+
+
+HELD = ("wp", "wo", "w_adapt", "wg", "wd", "inputs", "tab", "noise", "fw")
+
+
+def hold(n, name):
+    return pltpu.make_async_copy(getattr(n, name + "_i"), getattr(n, name), n.in_s.at[HELD.index(name)])
 
 
 def forward_body(n, z):
@@ -738,50 +753,51 @@
 
 def shapes_of(z):
     rowed = (z.N, z.R, z.CT, D)
-    return {
-        "one": (rowed, bf16),
-        "two": (rowed, bf16),
-        "gf": (rowed, bf16),
-        "gb": (rowed, bf16),
-        "sb": (rowed, bf16),
-        "rsr": ((z.N, z.R - 1, z.CT, D), bf16),
-        "Wp": ((z.C, z.DR, 3 * z.HW), bf16),
-        "Wo": ((z.C, z.DR, z.HW), bf16),
-        "Wg": ((z.C, z.DR, 2 * z.FH), bf16),
-        "Wd": ((z.C, z.DR, z.FH), bf16),
-        "Wh": ((z.C, z.DR, z.PF), bf16),
-        "q": ((z.HD, z.N, z.W, HSIZE), bf16),
-        "k": ((z.HD, z.N, z.W, HSIZE), bf16),
-        "v": ((z.HD, z.N, z.W, HSIZE), bf16),
-        "att": ((z.N, z.W, z.HW), f32),
-        "oh": ((z.HD, z.W, HSIZE), f32),
-        "lse": ((z.HD, z.N, 8, z.W), f32),
-        "gu": ((z.N, z.W, 2 * z.FH), bf16),
-        "act": ((z.N, z.W, z.FH), bf16),
-        "stream": ((z.T, D), f32),
-        "branch": ((z.T, D), f32),
-        "gmid": ((z.T, D), f32),
-        "mod": ((VECTORS, PAD, D), f32),
-        "gad": ((VECTORS, PAD, D), f32),
-        "ghead": ((D, z.PF), f32),
-        "loss": ((8, z.PF), f32),
-        "pre": ((z.C * PAD, z.LW), f32),
-        "cond": ((z.C * PAD, z.LW), bf16),
-        "lv": ((z.C, z.LR, z.LW), bf16),
-        "ea": ((z.C, PAD, TF), bf16),
-        "pq": ((z.R, z.C, z.PF // z.C, D // z.R), f32 if z.PF // z.C % 16 else bf16),
-        "hq": ((z.R, z.C, z.DR // z.R, z.PF), f32 if z.DR // z.R % 16 else bf16),
-        "pa": ((z.R, z.C * z.F, z.aw), f32),
-        "ra": ((z.R, z.C * z.F, z.aw), f32),
-        "rs": ((z.C, PAD, z.aw), f32),
-        "rb": ((z.C, PAD, z.aw), f32),
-        "ab": ((z.R, z.C * z.F, z.aw), f32),
-        "feed": ((z.CT, D), f32),
-        "hat": ((z.CT, D), f32),
-        "rstd": ((z.CT, 128), f32),
-        "end": ((z.CT, D), bf16),
-        "gend": ((z.CT, D), f32),
-    }
+    return dict(
+        one=(rowed, bf16),
+        two=(rowed, bf16),
+        gf=(rowed, bf16),
+        gb=(rowed, bf16),
+        sb=(rowed, bf16),
+        rsr=((z.N, z.R - 1, z.CT, D), bf16),
+        Wp=((z.C, z.DR, 3 * z.HW), bf16),
+        Wo=((z.C, z.DR, z.HW), bf16),
+        Wg=((z.C, z.DR, 2 * z.FH), bf16),
+        Wd=((z.C, z.DR, z.FH), bf16),
+        Wh=((z.C, z.DR, z.PF), bf16),
+        q=((z.HD, z.N, z.W, HSIZE), bf16),
+        k=((z.HD, z.N, z.W, HSIZE), bf16),
+        v=((z.HD, z.N, z.W, HSIZE), bf16),
+        att=((z.N, z.W, z.HW), f32),
+        oh=((z.HD, z.W, HSIZE), f32),
+        lse=((z.HD, z.N, 8, z.W), f32),
+        gu=((z.N, z.W, 2 * z.FH), bf16),
+        act=((z.N, z.W, z.FH), bf16),
+        stream=((z.T, D), f32),
+        branch=((z.T, D), f32),
+        gmid=((z.T, D), f32),
+        mod=((VECTORS, PAD, D), f32),
+        gad=((VECTORS, PAD, D), f32),
+        ghead=((D, z.PF), f32),
+        loss=((8, z.PF), f32),
+        weight=((8, z.PF), f32),
+        pre=((z.C * PAD, z.LW), f32),
+        cond=((z.C * PAD, z.LW), bf16),
+        lv=((z.C, z.LR, z.LW), bf16),
+        ea=((z.C, PAD, TF), bf16),
+        pq=((z.R, z.C, z.PF // z.C, D // z.R), f32 if z.PF // z.C % 16 else bf16),
+        hq=((z.R, z.C, z.DR // z.R, z.PF), f32 if z.DR // z.R % 16 else bf16),
+        pa=((z.R, z.C * z.F, z.aw), f32),
+        ra=((z.R, z.C * z.F, z.aw), f32),
+        rs=((z.C, PAD, z.aw), f32),
+        rb=((z.C, PAD, z.aw), f32),
+        ab=((z.R, z.C * z.F, z.aw), f32),
+        feed=((z.CT, D), f32),
+        hat=((z.CT, D), f32),
+        rstd=((z.CT, 128), f32),
+        end=((z.CT, D), bf16),
+        gend=((z.CT, D), f32),
+    )
 
 
 def vm(shapes, names):
@@ -790,7 +806,7 @@
 
 def forward_call(z, ins):
     sh = shapes_of(z)
-    direct = ("gad", "ghead", "loss", "pre", "cond", "ea")
+    direct = ("gad", "ghead", "loss", "weight", "pre", "cond", "ea")
     outs = {k: sh[k] for k in direct}
     outs.update({k + "_o": sh[k] for k in KEPT})
     rest = ["Wh", "oh", "sb", "rsr", "lv", "pq", "hq", "pa", "ra", "rs", "rb", "ab", "feed", "hat", "rstd", "end", "gend"]
@@ -803,7 +819,11 @@
     for k in ("one_s", "br_s", "two_s", "fd_s", "gf_s"):
         scratch[k] = dma((2, z.N, max(6, z.R)))
     scratch["ex_s"] = dma((len(KEPT),))
-    got = run(forward_body, z, 0, ins, {}, outs, scratch, [k + "_o" for k in KEPT], 60 << 20)
+    scratch["in_s"] = dma((len(HELD),))
+    scratch.update({k: pltpu.VMEM(ins[k].shape, ins[k].dtype) for k in HELD})
+    anys = {k + "_i": ins[k] for k in HELD}
+    ins = {k: v for k, v in ins.items() if k not in HELD}
+    got = run(forward_body, z, 0, ins, anys, outs, scratch, [k + "_o" for k in KEPT], 60 << 20)
     return {(k[:-2] if k.endswith("_o") else k): v for k, v in got.items()}
 
 
@@ -827,11 +847,11 @@
         "noise": noise.reshape(z.T, z.PF),
         "fw": jnp.broadcast_to(frame_weight[0][:, None, None], (z.F, z.LT, z.PF)).reshape(z.T, z.PF),
         "tab": jnp.asarray(rotary_consts(z)),
-    }, frame_weight
+    }
 
 
 def fetch(n, name):
-    i = LOADED.index(name)
+    i = (LOADED + LATER).index(name)
     return pltpu.make_async_copy(getattr(n, name + "_i"), getattr(n, name), n.in_s.at[i])
 
 
@@ -965,7 +985,7 @@
 
 
 def phase_pull_two(n, z):
-    for name in ("stream", "branch", "gmid"):
+    for name in ("stream", "branch", "gmid") + LATER:
         fetch(n, name).wait()
 
     def chunk(s, _):
@@ -978,11 +998,11 @@
             branch = n.branch[rows, :]
             hat, rstd = normed(n.stream[rows, :] + vec(n, 2, f) * branch)
             dx, d_shift, d_scale = norm_pull(hat, rstd, vec(n, 4, f), summed(n, z, c, i))
-            n.gadp[3, pl.ds(f, 1), :] = d_shift
-            n.gadp[4, pl.ds(f, 1), :] = d_scale
+            n.gad[3, pl.ds(f, 1), :] = d_shift
+            n.gad[4, pl.ds(f, 1), :] = d_scale
             mid = n.gmid[rows, :] + dx
             n.gmid[rows, :] = mid
-            n.gadp[2, pl.ds(f, 1), :] = jnp.sum(mid * branch, 0, keepdims=True)
+            n.gad[2, pl.ds(f, 1), :] = jnp.sum(mid * branch, 0, keepdims=True)
             n.gb[c, n.row, pl.ds(pl.multiple_of(i * z.LT, z.LT), z.LT), :] = (mid * vec(n, 2, f)).astype(bf16)
             return 0
 
@@ -1089,8 +1109,8 @@
             rows = frame_rows(z, c, i)
             hat, rstd = normed(n.stream[rows, :])
             dx, d_shift, d_scale = norm_pull(hat, rstd, vec(n, 1, f), summed(n, z, c, i))
-            n.gadp[0, pl.ds(f, 1), :] = d_shift
-            n.gadp[1, pl.ds(f, 1), :] = d_scale
+            n.gad[0, pl.ds(f, 1), :] = d_shift
+            n.gad[1, pl.ds(f, 1), :] = d_scale
             n.gb[c, n.row, pl.ds(pl.multiple_of(i * z.LT, z.LT), z.LT), :] = (n.gmid[rows, :] + dx).astype(bf16)
             return 0
 
@@ -1158,7 +1178,7 @@
     for r in range(z.R):
         for i in owners:
             col = i * z.AW + r * z.aw
-            n.xa[r, i] = n.gadp[col // D, :, col % D : col % D + z.aw]
+            n.xa[r, i] = n.gad[col // D, :, col % D : col % D + z.aw]
 
 
 def early_row(n, z):
@@ -1263,6 +1283,7 @@
 
 
 LOADED = ("Wd", "gu", "gf", "Wg", "stream", "branch", "gmid", "act", "two", "Wo", "q", "k", "v", "att", "lse", "Wp", "one")
+LATER = ("mod", "gad", "tab", "ghead", "w_adapt", "inputs", "cond", "ea", "pre")
 
 
 def reduce_start(n, z, x):
@@ -1293,11 +1314,10 @@
 
 
 def backward_body(n, z):
-    for name in LOADED:
+    for name in LOADED + LATER:
         if name not in ("one", "two"):
             fetch(n, name).start()
     n.squares[...] = jnp.zeros_like(n.squares)
-    n.gadp[...] = n.gad[...]
     if n.line:
         for k, p in enumerate(n.core_peer):
 
@@ -1353,48 +1373,50 @@
         stats=((8, 128), f32),
     )
     anys = {k + "_i": kept[k] for k in LOADED}
+    anys.update({k + "_i": ins[k] for k in LATER})
     scratch = vm(sh, [k for k in LOADED if k not in ("one", "two")] + ["gb", "sb", "rsr"])
+    scratch.update({k: pltpu.VMEM(ins[k].shape, ins[k].dtype) for k in LATER})
+    ins = {k: v for k, v in ins.items() if k not in LATER}
     for x, w in widths.items():
         scratch["S" + x] = pltpu.VMEM((z.C // 2, z.DR, w), bf16)
         scratch["R" + x] = pltpu.VMEM((z.C // 2 - 1, z.DR, w), bf16)
-    extra = {
-        "tb": ((D // max(2, z.W // 192), z.N * z.W), bf16),
-        "do": ((z.HD, z.W, HSIZE), bf16),
-        "delta": ((z.HD, 8, z.W), f32),
-        "dq": ((z.HD, z.W, HSIZE), f32),
-        "dkv": ((z.HD, z.N, z.W, 2 * HSIZE), f32),
-        "gp": ((z.N, z.W, 3 * z.HW), bf16),
-        "gadp": ((VECTORS, PAD, D), f32),
-        "squares": ((8, 128), f32),
-        "xa": ((z.R, z.C, PAD, z.aw), f32),
-        "ya": ((z.R, z.C, PAD, z.aw), f32),
-        "xp": ((z.R, z.PF, pw), bf16),
-        "yp": ((z.R, z.PF, pw), bf16),
-        "xh": ((z.R, z.C, hr, z.PF), head_type),
-        "yh": ((z.R, z.C, hr, z.PF), head_type),
-        "ca": ((z.C, PAD, z.aw), bf16),
-        "da": ((z.C, PAD, z.aw), bf16),
-        "cp": ((z.C, pr, pw), patch_type),
-        "dp": ((z.C, pr, pw), patch_type),
-        "ch": ((z.C, hr, z.PF), head_type),
-        "dh": ((z.C, hr, z.PF), head_type),
-        "ea2": ((z.R, z.C * PAD, z.aw), bf16),
-        "ep": ((z.R, pr, pw), f32),
-        "eh": ((z.R, hr, z.PF), f32),
-        "gc": ((z.C, PAD, z.LW), f32),
-        "gd": ((z.C, PAD, z.LW), f32),
-        "gl": ((z.C, PAD, z.LW), bf16),
-        "glv": ((TF, z.LW), f32),
-        "sa": ((z.R, 8, 128), f32),
-        "sc": ((z.C, 8, 128), f32),
-    }
+    extra = dict(
+        tb=((D // max(2, z.W // 192), z.N * z.W), bf16),
+        do=((z.HD, z.W, HSIZE), bf16),
+        delta=((z.HD, 8, z.W), f32),
+        dq=((z.HD, z.W, HSIZE), f32),
+        dkv=((z.HD, z.N, z.W, 2 * HSIZE), f32),
+        gp=((z.N, z.W, 3 * z.HW), bf16),
+        squares=((8, 128), f32),
+        xa=((z.R, z.C, PAD, z.aw), f32),
+        ya=((z.R, z.C, PAD, z.aw), f32),
+        xp=((z.R, z.PF, pw), bf16),
+        yp=((z.R, z.PF, pw), bf16),
+        xh=((z.R, z.C, hr, z.PF), head_type),
+        yh=((z.R, z.C, hr, z.PF), head_type),
+        ca=((z.C, PAD, z.aw), bf16),
+        da=((z.C, PAD, z.aw), bf16),
+        cp=((z.C, pr, pw), patch_type),
+        dp=((z.C, pr, pw), patch_type),
+        ch=((z.C, hr, z.PF), head_type),
+        dh=((z.C, hr, z.PF), head_type),
+        ea2=((z.R, z.C * PAD, z.aw), bf16),
+        ep=((z.R, pr, pw), f32),
+        eh=((z.R, hr, z.PF), f32),
+        gc=((z.C, PAD, z.LW), f32),
+        gd=((z.C, PAD, z.LW), f32),
+        gl=((z.C, PAD, z.LW), bf16),
+        glv=((TF, z.LW), f32),
+        sa=((z.R, 8, 128), f32),
+        sc=((z.C, 8, 128), f32),
+    )
     scratch.update(vm(extra, extra))
     dma = pltpu.SemaphoreType.DMA
     if z.C == 8:
         scratch["Xg"] = pltpu.VMEM((z.DR, 2 * z.FH), bf16)
         scratch["Xg_s"] = dma((2,))
     scratch["Rv_s"] = dma((2, z.C // 2))
-    scratch["in_s"] = dma((len(LOADED),))
+    scratch["in_s"] = dma((len(LOADED + LATER),))
     for x in widths:
         scratch["S" + x + "_s"] = dma((2, z.C // 2))
         scratch["R" + x + "_s"] = dma((2, z.C // 2))
@@ -1458,7 +1480,7 @@
 
 
 def adam_call(z, stats, grads, masters, firsts, seconds):
-    steps = 4
+    steps = 2
     split = (None, None, 0, 1, 0, 0, 0, 0)
 
     def spec(x, axis):
@@ -1486,12 +1508,10 @@
     a = dict(zip(["w_" + k for k in WEIGHTS], masters))
     a.update(latents=latents, noise=noise, levels=levels)
     z = sizes_of(latents, lax.axis_size("clip"), lax.axis_size("row"))
-    ins, frame_weight = forward_inputs(z, a)
+    ins = forward_inputs(z, a)
     kept = forward_call(z, ins)
-    weight = jnp.sum(frame_weight) * z.LT
-    back = {k: kept[k] for k in ("gad", "ghead", "loss", "pre", "cond", "ea", "mod")}
+    back = {k: kept[k] for k in ("gad", "ghead", "loss", "weight", "pre", "cond", "ea", "mod")}
     back.update({k: ins[k] for k in ("w_adapt", "inputs", "tab")})
-    back["weight"] = jnp.zeros((8, 128), f32).at[0, 0].set(weight)
     g = backward_call(z, kept, back)
     grads = (g["gpatch"], g["glevel"], g["gadapt"], g["Gp"], g["Go"], g["Gg"], g["Gd"], g["gheads"])
     scalars, *results = adam_call(z, g["stats"], grads, *(to_kernel(x) for x in (masters, firsts, seconds)))

time: 315 us -> 310 us (0.984)
  no operation moved by 1% of the time
where the time goes in v3:
time: 310 us
  Pallas kernels  304 us (98%)
  other arithmetic  3.88 us (1%)
    pallas_call x2, Pallas kernels, run(): pl.pallas_call(kernel, out_shape=[jax.ShapeDtypeStruct(s, d) for s, d in...  293 us
    pallas_call x1, Pallas kernels, adam_call(): pl.pallas_call(functools.partial(adam_kernel, z.PF), grid=(steps,), out_s...  10.8 us

profile of v3, /device:TPU:0, one launch (start us, length us, event | category | flops | bytes accessed | tf_op | source)
XLA Modules:
  0.0 310.1 jit_solution(5991175689289989477)
XLA Ops:
  0.7 0.7 convert_bitcast_fusion
  1.3 0.7 minimum_bitcast_fusion
  2.1 0.1 fusion.4
  2.2 0.6 fusion.6.refs_0_
  2.8 0.1 mul.60
  2.9 0.1 mul.61
  2.9 0.1 broadcast_in_dim.14
  3.0 0.1 broadcast_in_dim.15
  3.1 0.1 mul.65
  3.2 0.1 mul.66
  3.2 1.8 fusion.1.refs_9_.refs_24_
  5.0 0.8 broadcast_in_dim.16.refs_12_
  5.8 146.7 %shard_map.475 = (f32[8,16,1024]{2,1,0:T(8,128)}, f32[1024,128]{1,0:T(8,128)}, f32[8,128]{1,0:T(8,128)}, f32[8,128]{1,0:T(8,128)}, f32[128,256]{1,0:T(8,128)}, /...) custom-call(bf16[16,256]{1,0:T(8,128)(2,1)} %fusion.6.refs_0_, ...), custom_call_target="tpu_custom_call" | custom-call | tf_op jit(solution)/shard_map/pallas_call | solution.py:709
  152.5 146.7 %shard_map.476 = (f32[3,128,256]{2,1,0:T(8,128)}, f32[256,128]{1,0:T(8,128)}, f32[2048,128]{1,0:T(8,128)}, f32[1024,128]{1,0:T(8,128)}, f32[16,1024]{1,0:T(8,128...) custom-call(f32[8,128]{1,0:T(8,128)} %get-tuple-element.88.refs_0_, ...), custom_call_target="tpu_custom_call" | custom-call | tf_op jit(solution)/shard_map/pallas_call | solution.py:709
  299.2 10.8 %shard_map.477 = (f32[1,1]{1,0:T(1,128)}, f32[1,1]{1,0:T(1,128)}, f32[1,1]{1,0:T(1,128)}, f32[16,1024]{1,0:T(8,128)}, f32[32,256]{1,0:T(8,128)}, /*index=5*/f32[...) custom-call(f32[8,128]{1,0:T(8,128)} %get-tuple-element.113.stats, ...), custom_call_target="tpu_custom_call" | custom-call | tf_op jit(solution)/shard_map/pallas_call | solution.py:1495
  (2 shorter events, 0.0 us)

commit v4 on v3

--- a/solution.py
+++ b/solution.py
@@ -897,7 +897,7 @@
 def weight_grad(n, z, left, right, into):
     half = n.tb.shape[0]
     width = right.shape[-1]
-    tile = min(256, width)
+    tile = next(t for t in (512, 256, 128) if width % t == 0)
     slabs = half // z.DR
     for part in range(D // half):
         for c in range(z.N):

time: 310 us -> 309 us (level)
  no operation moved by 1% of the time
where the time goes in v4:
time: 309 us
  Pallas kernels  303 us (98%)
  other arithmetic  3.88 us (1%)
    pallas_call x2, Pallas kernels, run(): pl.pallas_call(kernel, out_shape=[jax.ShapeDtypeStruct(s, d) for s, d in...  292 us
    pallas_call x1, Pallas kernels, adam_call(): pl.pallas_call(functools.partial(adam_kernel, z.PF), grid=(steps,), out_s...  10.8 us

profile of v4, /device:TPU:0, one launch (start us, length us, event | category | flops | bytes accessed | tf_op | source)
XLA Modules:
  0.0 308.7 jit_solution(10614434135727843895)
XLA Ops:
  0.7 0.7 convert_bitcast_fusion
  1.3 0.7 minimum_bitcast_fusion
  2.1 0.1 fusion.4
  2.2 0.6 fusion.6.refs_0_
  2.8 0.1 mul.60
  2.9 0.1 mul.61
  2.9 0.1 broadcast_in_dim.14
  3.0 0.1 broadcast_in_dim.15
  3.1 0.1 mul.65
  3.2 0.1 mul.66
  3.2 1.8 fusion.1.refs_9_.refs_24_
  5.0 0.8 broadcast_in_dim.16.refs_12_
  5.8 146.7 %shard_map.475 = (f32[8,16,1024]{2,1,0:T(8,128)}, f32[1024,128]{1,0:T(8,128)}, f32[8,128]{1,0:T(8,128)}, f32[8,128]{1,0:T(8,128)}, f32[128,256]{1,0:T(8,128)}, /...) custom-call(bf16[16,256]{1,0:T(8,128)(2,1)} %fusion.6.refs_0_, ...), custom_call_target="tpu_custom_call" | custom-call | tf_op jit(solution)/shard_map/pallas_call | solution.py:709
  152.5 145.2 %shard_map.476 = (f32[3,128,256]{2,1,0:T(8,128)}, f32[256,128]{1,0:T(8,128)}, f32[2048,128]{1,0:T(8,128)}, f32[1024,128]{1,0:T(8,128)}, f32[16,1024]{1,0:T(8,128...) custom-call(f32[8,128]{1,0:T(8,128)} %get-tuple-element.88.refs_0_, ...), custom_call_target="tpu_custom_call" | custom-call | tf_op jit(solution)/shard_map/pallas_call | solution.py:709
  297.7 10.8 %shard_map.477 = (f32[1,1]{1,0:T(1,128)}, f32[1,1]{1,0:T(1,128)}, f32[1,1]{1,0:T(1,128)}, f32[16,1024]{1,0:T(8,128)}, f32[32,256]{1,0:T(8,128)}, /*index=5*/f32[...) custom-call(f32[8,128]{1,0:T(8,128)} %get-tuple-element.113.stats, ...), custom_call_target="tpu_custom_call" | custom-call | tf_op jit(solution)/shard_map/pallas_call | solution.py:1495
  (2 shorter events, 0.0 us)
